TPU v7x, 128 devices: a whole 4x4x4 slice. The times are simulated.
128 devices in a mesh: pts: 16 (over x, z), comp: 8 (over y, core).
Axes of the slice: x: 4, y: 4, z: 4, core: 2. Of those that a mesh axis runs over, the one named last changes fastest.
Arguments:
- spectrum: float32 [1152, 16384], P(None, ('pts', 'comp')), may hold values from 0.05 to 4
- turning: float32 [1152, 16384], P(None, ('pts', 'comp')), may hold values from -0.45 to 0.45
- courant_x: float32 [1152, 16384], P(('pts', 'comp')), may hold values from -0.45 to 0.45
- courant_y: float32 [1152, 16384], P(('pts', 'comp')), may hold values from -0.45 to 0.45
- neighbors: int32 [4, 16384], replicated, may hold values from 0 to 16383, as said below
- nest_spectra: float32 [13312, 1152], P(('pts', 'comp')), may hold values from 0.05 to 4
- nest_owner: int32 [13312, 1], P(('pts', 'comp')), may hold values from 0 to 127; in each aligned block of 104 rows (0 to 103, 104 to 207, ...) at most 4 rows name the same one
- nest_point: int32 [13312], P(('pts', 'comp')), may hold values from 0 to 127, as said below
- nest_weight: float32 [13312], P(('pts', 'comp')), may hold values from 0.02 to 1
Outputs:
- spectrum_next: float32 [1152, 16384], P(None, ('pts', 'comp'))
Inputs may be any that keep to these rules, and one draw needn't show every extreme that they name: `neighbors`: rows are the west, east, south and north neighbours of each sea point on a grid 128 points wide in point order, or the point itself where the neighbour is land or outside. `nest_owner`: among the rows of one device no owner is named more than 4 times. `nest_point`: each row names the west or the east end of its owner's grid row: 0 or 127.
All inputs are finite; a program needn't handle non-finite values.
Results may differ from a plain program's by a relative error of at most 0.0003.
Values sent between devices are 32-bit elements; how exact they have to be, the bound alone decides.
A program may use at most 64 MiB of HBM per device.

v0:
```python
import jax
import jax.numpy as jnp
from jax import lax
from jax.sharding import PartitionSpec as P

NTH = 36
CAP = 4
REF_SUB = 2
ADV_SUB = 3


def refract(energy, rates):
    upstream = jnp.roll(energy, -1, axis=1)
    fluxes = jnp.maximum(rates, 0.0) * energy + jnp.minimum(rates, 0.0) * upstream
    return energy - fluxes + jnp.roll(fluxes, 1, axis=1)


def pick_upwind(energy, upwind, position, stride):
    before = jnp.roll(energy, stride, axis=1)
    after = jnp.roll(energy, -stride, axis=1)
    return jnp.where(
        upwind == position - stride, before, jnp.where(upwind == position + stride, after, energy)
    )


def advect(energy, speed_x, speed_y, upwind_x, upwind_y, position, row_width):
    from_x = pick_upwind(energy, upwind_x, position, 1)
    from_y = pick_upwind(energy, upwind_y, position, row_width)
    return energy - jnp.abs(speed_x) * (energy - from_x) - jnp.abs(speed_y) * (energy - from_y)


def body(
    spectrum,
    turning,
    courant_x,
    courant_y,
    neighbors,
    nest_spectra,
    nest_owner,
    nest_point,
    nest_weight,
):
    components, point_count = spectrum.shape
    pts_count = lax.axis_size("pts")
    comp_count = lax.axis_size("comp")
    devices = pts_count * comp_count
    per_device = components // devices
    all_points = devices * point_count
    row_count = nest_spectra.shape[0]
    energy = spectrum.reshape(components // NTH, NTH, point_count)
    rates = turning.reshape(components // NTH, NTH, point_count)
    for substep in range(REF_SUB):
        energy = refract(energy, rates)
    energy = energy.reshape(components, point_count)
    blocks = energy.reshape(devices, per_device, point_count)
    moved = lax.all_to_all(blocks, ("pts", "comp"), split_axis=0, concat_axis=2, tiled=True)
    energy = moved.reshape(per_device, all_points)
    position = jnp.arange(all_points, dtype=jnp.int32)[None, :]
    upwind_x = jnp.where(courant_x > 0, neighbors[0][None, :], neighbors[1][None, :])
    upwind_y = jnp.where(courant_y > 0, neighbors[2][None, :], neighbors[3][None, :])
    for substep in range(ADV_SUB):
        energy = advect(energy, courant_x, courant_y, upwind_x, upwind_y, position, point_count)
    weighted = nest_spectra * nest_weight[:, None]
    owner_ids = nest_owner[:, 0]
    blocks = energy.reshape(per_device, devices, point_count)
    moved = lax.all_to_all(blocks, ("pts", "comp"), split_axis=1, concat_axis=0, tiled=True)
    energy = moved.reshape(components, point_count)
    row_index = jnp.arange(row_count, dtype=jnp.int32)
    same_owner = owner_ids[:, None] == owner_ids[None, :]
    earlier = jnp.logical_and(same_owner, row_index[None, :] < row_index[:, None])
    rank_index = jnp.sum(earlier.astype(jnp.int32), axis=1)
    slot_index = owner_ids * CAP + rank_index
    slot_count = devices * CAP
    slot_table = (jnp.arange(slot_count, dtype=jnp.int32)[:, None] == slot_index[None, :]).astype(
        jnp.float32
    )
    packed = jnp.dot(slot_table, weighted, precision=lax.Precision.HIGHEST)
    packed_weight = jnp.dot(slot_table, nest_weight, precision=lax.Precision.HIGHEST)
    packed_point = jnp.dot(
        slot_table, nest_point.astype(jnp.float32), precision=lax.Precision.HIGHEST
    )
    got_rows, got_weight, got_point = (
        lax.all_to_all(packed, ("pts", "comp"), split_axis=0, concat_axis=0, tiled=True),
        lax.all_to_all(packed_weight, ("pts", "comp"), split_axis=0, concat_axis=0, tiled=True),
        lax.all_to_all(packed_point, ("pts", "comp"), split_axis=0, concat_axis=0, tiled=True),
    )
    point_table = (
        got_point.astype(jnp.int32)[:, None] == jnp.arange(point_count, dtype=jnp.int32)[None, :]
    ).astype(jnp.float32)
    added_energy = lax.dot_general(
        got_rows, point_table, (((0,), (0,)), ((), ())), precision=lax.Precision.HIGHEST
    )
    total_weight = jnp.dot(got_weight, point_table, precision=lax.Precision.HIGHEST)
    energy = (energy + added_energy) / (1.0 + total_weight)[None, :]
    return energy


def solution(mesh):
    placed = (
        P(None, ("pts", "comp")),
        P(None, ("pts", "comp")),
        P(("pts", "comp"), None),
        P(("pts", "comp"), None),
        P(),
        P(("pts", "comp"), None),
        P(("pts", "comp"), None),
        P(("pts", "comp")),
        P(("pts", "comp")),
    )
    return jax.shard_map(
        body, mesh=mesh, in_specs=placed, out_specs=P(None, ("pts", "comp")), check_vma=False
    )
```

profile of v0, /device:TPU:1, one launch (start us, length us, event | category | flops | bytes accessed | tf_op | source)
XLA Modules:
  0.0 156.8 jit_solution(12465277170194487343)
XLA Ops:
  0.0 1.2 reshape.75
  1.2 0.9 slice.156
  2.1 0.1 broadcast_maximum_fusion
  2.2 0.0 copy-start.2
  2.3 2.2 %multiply_add_fusion.1 = (f32[32,36,128]{2,1,0:T(8,128)S(1)}, f32[32,36,128]{2,1,0:T(8,128)}) fusion(f32[32,36,128]{2,1,0:T(8,128)S(1)} %min.13, f32[32,36,128]{2,1,0:T(8,128)S(1)} %max.13, f32[32,36,128]{2,1,0:T(8,128)S(1)} %reshape.75, f32[32,1,128]{2,1,0:T(1,128)S(1)} %slice.157, f32[32,35,128]{2,1,0:T(8,128)} %slice.156), kind=kLoop, calls=%fused_computation.45 | loop fusion | flops 589824 | bytes 3538944 | tf_op jit(solution)/shard_map/add | solution.py:14
  4.5 1.0 subtract_add_fusion.1
  5.6 2.1 %max.12 = f32[128,9,128]{2,1,0:T(8,128)} reshape(f32[1152,128]{1,0:T(8,128)} %copy-done.2) | data formatting | bytes 1179648 | tf_op jit(solution)/shard_map/max | solution.py:14
  7.7 1.0 min.12
  8.8 2.1 %reshape.74 = f32[128,9,128]{2,1,0:T(8,128)} reshape(f32[1152,128]{1,0:T(8,128)} %param.9) | data formatting | bytes 1179648 | tf_op jit(solution)/shard_map/reshape | solution.py:50
  10.9 1.0 multiply_add_fusion
  11.9 0.1 pad_maximum_fusion.3
  11.9 1.1 concatenate.69
  13.0 2.3 %concatenate.67 = f32[128,9,128]{2,1,0:T(8,128)} reshape(f32[32,36,128]{2,1,0:T(8,128)} %get-tuple-element.6) | data formatting | bytes 1179648 | tf_op jit(solution)/shard_map/jit(_roll_static)/concatenate | solution.py:13
  15.3 2.2 %concatenate.65 = f32[128,9,128]{2,1,0:T(8,128)} reshape(f32[32,36,128]{2,1,0:T(8,128)} %get-tuple-element.8) | data formatting | bytes 1179648 | tf_op jit(solution)/shard_map/jit(_roll_static)/concatenate | solution.py:15
  17.5 2.1 %concatenate.63 = f32[128,9,128]{2,1,0:T(8,128)} reshape(f32[32,36,128]{2,1,0:T(8,128)} %get-tuple-element.10) | data formatting | bytes 1179648 | tf_op jit(solution)/shard_map/jit(_roll_static)/concatenate | solution.py:13
  19.6 0.0 copy-start.10
  19.6 3.7 %subtract_add_fusion = f32[128,9,128]{2,1,0:T(8,128)} fusion(f32[128,9,128]{2,1,0:T(8,128)} %concatenate.69, f32[128,9,128]{2,1,0:T(8,128)S(1)} %copy-done.4, f32[128,9,128]{2,1,0:T(8,128)} %concatenate.67, f32[128,9,128]{2,1,0:T(8,128)S(1)} %copy-done.3, f32[128,9,128]{2,1,0:T(8,128)} %concatenate.65, f32[128,9,128]{2,1,0:T(8,128)S(1)} %copy-done.5, ...), kind=kLoop, calls=%fused_computation.38 | loop fusion | flops 1474560 | bytes 4718592 | tf_op jit(solution)/shard_map/add | solution.py:15
  23.3 11.5 %all-to-all-start = ((f32[128,9,128]{2,1,0:T(8,128)}), f32[128,9,128]{2,1,0:T(8,128)S(1)}, u32[]{:S(2)}, u32[]{:S(2)}) async-start(f32[128,9,128]{2,1,0:T(8,128)} %subtract_add_fusion), calls=%async_computation | async-start | bytes 2097152 | tf_op jit(solution)/shard_map/all_to_all | solution.py:56
  34.8 0.8 fusion.46
  35.7 0.2 convert_reduce_fusion.1
  35.9 0.2 fusion.23
  36.1 0.7 all_to_all.53
  36.8 0.2 fusion.22
  37.1 0.7 all_to_all.55
  37.9 16.0 %all-to-all-done = f32[128,9,128]{2,1,0:T(8,128)S(1)} async-done(((f32[128,9,128]{2,1,0:T(8,128)}), f32[128,9,128]{2,1,0:T(8,128)S(1)}, u32[]{:S(2)}, u32[]{:S(2)}) %all-to-all-start) | async-done | bytes 589856 | tf_op jit(solution)/shard_map/all_to_all | solution.py:56
  53.9 5.5 %all-to-all-start.3 = ((f32[128,4,1]{1,2,0:T(1,128)}), f32[128,4,1]{1,2,0:T(1,128)}, u32[]{:S(2)}, u32[]{:S(2)}) async-start(f32[128,4,1]{1,2,0:T(1,128)} %bitcast.11), calls=%async_computation.3 | async-start | bytes 131072 | tf_op jit(solution)/shard_map/all_to_all | solution.py:85
  59.4 0.2 copy.31
  59.6 0.1 pad.32
  59.7 0.6 copy.28
  60.3 0.3 fusion.44
  60.7 0.0 copy-start.1
  60.7 0.1 fusion.42
  60.8 0.1 fusion.45
  60.9 1.0 copy-done
  61.9 0.3 copy-done.1
  62.2 1.0 fusion.5
  63.2 0.3 fusion.40
  63.5 0.1 fusion.38
  63.7 0.1 fusion.41
  63.7 1.0 fusion.11
  64.7 1.6 %fusion.36 = (f32[9,16383]{1,0:T(8,128)}, f32[9,16383]{1,0:T(8,128)}) fusion(f32[9,16384]{1,0:T(8,128)S(1)} %fusion.11), kind=kLoop, calls=%fused_computation.75 | loop fusion | bytes 2359152 | tf_op jit(solution)/shard_map/jit(_roll_static)/slice | solution.py:20
  66.3 1.5 fusion.34
  67.8 0.7 fusion.37
  68.5 0.3 all-to-all-done.3
  68.8 10.0 %all-to-all-start.4 = ((f32[128,4,1]{1,2,0:T(1,128)}), f32[128,4,1]{1,2,0:T(1,128)}, u32[]{:S(2)}, u32[]{:S(2)}) async-start(f32[128,4,1]{1,2,0:T(1,128)} %bitcast.67), calls=%async_computation.4 | async-start | bytes 131072 | tf_op jit(solution)/shard_map/all_to_all | solution.py:84
  78.8 3.0 %fusion.17 = f32[9,16384]{1,0:T(8,128)S(1)} fusion(f32[9,16384]{1,0:T(8,128)S(1)} %fusion.11, f32[9,16383]{1,0:T(8,128)} %get-tuple-element.16, f32[9,1]{1,0:T(8,128)} %get-tuple-element.18, f32[9,1]{1,0:T(8,128)} %get-tuple-element.17, f32[9,16383]{1,0:T(8,128)} %get-tuple-element.15, f32[9,16256]{1,0:T(8,128)} %get-tuple-element.12, ...), kind=kLoop, calls=%fused_computation.32 | loop fusion | flops 3538944 | bytes 5242880 | tf_op jit(solution)/shard_map/sub | solution.py:29
  81.8 0.2 copy.29
  82.1 1.3 copy.25
  83.5 4.8 %all-to-all-done.4 = f32[128,4,1]{1,2,0:T(1,128)} async-done(((f32[128,4,1]{1,2,0:T(1,128)}), f32[128,4,1]{1,2,0:T(1,128)}, u32[]{:S(2)}, u32[]{:S(2)}) %all-to-all-start.4) | async-done | bytes 2080 | tf_op jit(solution)/shard_map/all_to_all | solution.py:84
  88.2 5.0 %all-to-all-start.1 = ((f32[9,128,128]{2,0,1:T(8,128)}), f32[9,128,128]{2,0,1:T(8,128)S(1)}, u32[]{:S(2)}, u32[]{:S(2)}) async-start(f32[9,128,128]{2,0,1:T(8,128)} %copy.25), calls=%async_computation.1 | async-start | bytes 2097152 | tf_op jit(solution)/shard_map/all_to_all | solution.py:66
  93.3 2.2 %fusion.20 = f32[512,1152]{1,0:T(8,128)S(1)} fusion(f32[104,1152]{1,0:T(8,128)} %param.14, f32[104]{0:T(128)S(1)} %copy-done.12, s32[104]{0:T(128)S(1)} %copy-done.14), kind=kOutput, calls=%fused_computation.47 | convolution fusion | flops 736273408 | bytes 2839360 | tf_op jit(solution)/shard_map/dot_general | solution.py:77
  95.5 1.8 %all_to_all.50 = f32[128,4,1152]{2,1,0:T(4,128)} reshape(f32[512,1152]{1,0:T(8,128)S(1)} %fusion.20) | data formatting | bytes 4718592 | tf_op jit(solution)/shard_map/all_to_all | solution.py:83
  97.3 15.1 %all-to-all-done.1 = f32[9,128,128]{2,0,1:T(8,128)S(1)} async-done(((f32[9,128,128]{2,0,1:T(8,128)}), f32[9,128,128]{2,0,1:T(8,128)S(1)}, u32[]{:S(2)}, u32[]{:S(2)}) %all-to-all-start.1) | async-done | bytes 589856 | tf_op jit(solution)/shard_map/all_to_all | solution.py:66
  112.3 4.7 %all-to-all-start.2 = ((f32[128,4,1152]{2,1,0:T(4,128)}), f32[128,4,1152]{2,1,0:T(4,128)S(1)}, u32[]{:S(2)}, u32[]{:S(2)}) async-start(f32[128,4,1152]{2,1,0:T(4,128)} %all_to_all.50), calls=%async_computation.2 | async-start | bytes 4718592 | tf_op jit(solution)/shard_map/all_to_all | solution.py:83
  117.0 1.0 convert_reduce_fusion
  118.0 0.1 convert_element_type.21
  118.2 0.5 broadcast.73
  118.7 1.6 %reduce.7 = f32[128,4]{1,0:T(8,128)S(1)} reduce(f32[128,4,1]{1,2,0:T(1,128)} %all-to-all-done.4, f32[]{:T(128)} %broadcast.73), dimensions={2}, to_apply=%all_to_all.56.reduce_sub_computation.3 | reduce | bytes 4100 | tf_op jit(solution)/shard_map/all_to_all | solution.py:84
  120.3 0.1 reshape.83
  120.4 0.3 fusion.1
  120.7 0.9 reshape.78
  121.6 28.7 %all-to-all-done.2 = f32[128,4,1152]{2,1,0:T(4,128)S(1)} async-done(((f32[128,4,1152]{2,1,0:T(4,128)}), f32[128,4,1152]{2,1,0:T(4,128)S(1)}, u32[]{:S(2)}, u32[]{:S(2)}) %all-to-all-start.2) | async-done | bytes 2359328 | tf_op jit(solution)/shard_map/all_to_all | solution.py:83
  150.4 1.8 %all_to_all.52 = f32[512,1152]{1,0:T(8,128)} reshape(f32[128,4,1152]{2,1,0:T(4,128)S(1)} %all-to-all-done.2) | data formatting | bytes 4718592 | tf_op jit(solution)/shard_map/all_to_all | solution.py:83
  152.2 4.6 %fusion = f32[1152,128]{1,0:T(8,128)} fusion(f32[1152,128]{1,0:T(8,128)S(1)} %copy-done.6, f32[512,1152]{1,0:T(8,128)} %all_to_all.52, f32[128]{0:T(128)S(1)} %fusion.1, s32[512]{0:T(512)S(1)} %convert_element_type.21), kind=kOutput, calls=%fused_computation.1 | convolution fusion | flops 906330112 | bytes 3541504 | tf_op jit(solution)/shard_map/dot_general | solution.py:90
  (43 shorter events, 0.3 us)
Async XLA Ops:
  0.0 2.1 %copy-start.9 = (f32[1152,128]{1,0:T(8,128)S(1)}, f32[1152,128]{1,0:T(8,128)}, u32[]{:S(2)}) copy-start(f32[1152,128]{1,0:T(8,128)} %param.10) | copy-start | bytes 1769476
  2.2 2.4 %copy-start.2 = (f32[1152,128]{1,0:T(8,128)}, f32[1152,128]{1,0:T(8,128)S(1)}, u32[]{:S(2)}) copy-start(f32[1152,128]{1,0:T(8,128)S(1)} %get-tuple-element.35) | copy-start | bytes 1769476
  13.0 6.5 %copy-start.3 = (f32[128,9,128]{2,1,0:T(8,128)S(1)}, f32[128,9,128]{2,1,0:T(8,128)}, u32[]{:S(2)}) copy-start(f32[128,9,128]{2,1,0:T(8,128)} %max.12) | copy-start | bytes 1769476
  13.0 6.5 %copy-start.4 = (f32[128,9,128]{2,1,0:T(8,128)S(1)}, f32[128,9,128]{2,1,0:T(8,128)}, u32[]{:S(2)}) copy-start(f32[128,9,128]{2,1,0:T(8,128)} %min.12) | copy-start | bytes 1769476
  13.0 6.5 %copy-start.5 = (f32[128,9,128]{2,1,0:T(8,128)S(1)}, f32[128,9,128]{2,1,0:T(8,128)}, u32[]{:S(2)}) copy-start(f32[128,9,128]{2,1,0:T(8,128)} %reshape.74) | copy-start | bytes 1769476
  19.6 15.2 %copy-start.10 = (s32[4,16384]{1,0:T(4,128)S(1)}, s32[4,16384]{1,0:T(4,128)}, u32[]{:S(2)}) copy-start(s32[4,16384]{1,0:T(4,128)} %param.13) | copy-start | bytes 786436
  23.3 12.4 %copy-start.15 = (s32[104,1]{0,1:T(1,128)S(1)}, s32[104,1]{0,1:T(1,128)}, u32[]{:S(2)}) copy-start(s32[104,1]{0,1:T(1,128)} %param.15) | copy-start | bytes 1252
  23.3 12.5 %copy-start.16 = (s32[104]{0:T(128)S(1)}, s32[104]{0:T(128)}, u32[]{:S(2)}) copy-start(s32[104]{0:T(128)} %param.16) | copy-start | bytes 1252
  23.3 13.5 %copy-start.11 = (f32[104]{0:T(128)S(1)}, f32[104]{0:T(128)}, u32[]{:S(2)}) copy-start(f32[104]{0:T(128)} %param.17) | copy-start | bytes 1252
  23.3 30.6 %all-to-all-start = ((f32[128,9,128]{2,1,0:T(8,128)}), f32[128,9,128]{2,1,0:T(8,128)S(1)}, u32[]{:S(2)}, u32[]{:S(2)}) async-start(f32[128,9,128]{2,1,0:T(8,128)} %subtract_add_fusion), calls=%async_computation | async-start | bytes 2097152 | tf_op jit(solution)/shard_map/all_to_all | solution.py:56
  35.9 24.4 %copy-start.13 = (s32[104]{0:T(128)}, s32[104]{0:T(128)S(1)}, u32[]{:S(2)}) copy-start(s32[104]{0:T(128)S(1)} %multiply_add_fusion.2) | copy-start | bytes 1252
  53.9 14.9 %all-to-all-start.3 = ((f32[128,4,1]{1,2,0:T(1,128)}), f32[128,4,1]{1,2,0:T(1,128)}, u32[]{:S(2)}, u32[]{:S(2)}) async-start(f32[128,4,1]{1,2,0:T(1,128)} %bitcast.11), calls=%async_computation.3 | async-start | bytes 131072 | tf_op jit(solution)/shard_map/all_to_all | solution.py:85
  60.6 1.2 copy-start
  60.7 1.5 copy-start.1
  60.7 1.5 copy-start.7
  60.7 1.5 copy-start.8
  68.8 19.4 %all-to-all-start.4 = ((f32[128,4,1]{1,2,0:T(1,128)}), f32[128,4,1]{1,2,0:T(1,128)}, u32[]{:S(2)}, u32[]{:S(2)}) async-start(f32[128,4,1]{1,2,0:T(1,128)} %bitcast.67), calls=%async_computation.4 | async-start | bytes 131072 | tf_op jit(solution)/shard_map/all_to_all | solution.py:84
  82.1 11.2 %copy-start.12 = (f32[104]{0:T(128)S(1)}, f32[104]{0:T(128)}, u32[]{:S(2)}) copy-start(f32[104]{0:T(128)} %param.17) | copy-start | bytes 1252
  82.1 11.2 %copy-start.14 = (s32[104]{0:T(128)S(1)}, s32[104]{0:T(128)}, u32[]{:S(2)}) copy-start(s32[104]{0:T(128)} %copy-done.13) | copy-start | bytes 1252
  88.2 24.1 %all-to-all-start.1 = ((f32[9,128,128]{2,0,1:T(8,128)}), f32[9,128,128]{2,0,1:T(8,128)S(1)}, u32[]{:S(2)}, u32[]{:S(2)}) async-start(f32[9,128,128]{2,0,1:T(8,128)} %copy.25), calls=%async_computation.1 | async-start | bytes 2097152 | tf_op jit(solution)/shard_map/all_to_all | solution.py:66
  112.3 38.0 %all-to-all-start.2 = ((f32[128,4,1152]{2,1,0:T(4,128)}), f32[128,4,1152]{2,1,0:T(4,128)S(1)}, u32[]{:S(2)}, u32[]{:S(2)}) async-start(f32[128,4,1152]{2,1,0:T(4,128)} %all_to_all.50), calls=%async_computation.2 | async-start | bytes 4718592 | tf_op jit(solution)/shard_map/all_to_all | solution.py:83
  121.6 30.6 %copy-start.6 = (f32[1152,128]{1,0:T(8,128)S(1)}, f32[1152,128]{1,0:T(8,128)}, u32[]{:S(2)}) copy-start(f32[1152,128]{1,0:T(8,128)} %reshape.78) | copy-start | bytes 1769476
where the time goes:
time: 158 us; the launch traced here: 157 us
  waiting for transfers between devices  64.9 us (41%)
  starting transfers between devices  36.7 us (23%)
  local copies, waits for them, and re-layouts  31.4 us (20%)
  other arithmetic  15.8 us (10%)
  matrix products  7.53 us (5%)
    all_to_all x1, waiting for transfers between devices, body(): lax.all_to_all(packed, ('pts', 'comp'), split_axis=0, concat_axis=0, tile...  28.7 us
    all_to_all x1, waiting for transfers between devices, body(): lax.all_to_all(blocks, ('pts', 'comp'), split_axis=0, concat_axis=2, tile...  16 us
    all_to_all x1, waiting for transfers between devices, body(): lax.all_to_all(blocks, ('pts', 'comp'), split_axis=1, concat_axis=0, tile...  15.1 us
    all_to_all x1, starting transfers between devices, body(): lax.all_to_all(blocks, ('pts', 'comp'), split_axis=0, concat_axis=2, tile...  11.5 us
    all_to_all x1, starting transfers between devices, body(): lax.all_to_all(packed_weight, ('pts', 'comp'), split_axis=0, concat_axis=...  10 us
    all_to_all x1, starting transfers between devices, body(): lax.all_to_all(packed_point, ('pts', 'comp'), split_axis=0, concat_axis=0...  5.49 us
    all_to_all x1, starting transfers between devices, body(): lax.all_to_all(blocks, ('pts', 'comp'), split_axis=1, concat_axis=0, tile...  5.02 us
    sub x3, other arithmetic, advect(): energy - jnp.abs(speed_x) * (energy - from_x)  4.93 us
  transfers between devices with their start and end apart: 5, of which 5 were waited for; matrix products, arithmetic and copies ran while one was open for 13% of the time, Pallas kernels for 0%

commit v1 on v0

v1 whole, which is shorter than its diff:
```python
import functools

import jax
import jax.numpy as jnp
from jax import lax
from jax.experimental import pallas as pl
from jax.experimental.pallas import tpu as pltpu
from jax.sharding import PartitionSpec as P

MESH = pl.DeviceIdType.MESH
NTH = 36
CAP = 4
REF_SUB = 2
ADV_SUB = 3
PAD = 16
DMA = pltpu.SemaphoreType.DMA
CHUNKS = ((0, 9),)


def away(at, step):
    return (at + step * (1 - 2 * (at % 2)) + 4) % 4


def peer(i, pts, comp):
    x, z, y, core = pts // 4, pts % 4, comp // 2, comp % 2
    to_x, to_z = away(x, i // 32), away(z, (i // 8) % 4)
    to_y, to_core = away(y, (i // 2) % 4), (core + i) % 2
    return to_x * 4 + to_z, to_y * 2 + to_core


def refract(x, r, tmp, send):
    @pl.loop(0, x.shape[0] // (8 * NTH))
    def _(group):
        base = pl.multiple_of(group * (8 * NTH), 8)

        def substep(load, store):
            def flux(d):
                rate = r[pl.ds(base + d, 8, stride=NTH), :]
                return jnp.maximum(rate, 0.0) * load(d) + jnp.minimum(rate, 0.0) * load((d + 1) % NTH)

            before = flux(NTH - 1)
            for d in range(NTH):
                now = flux(d)
                store(d, load(d) - now + before)
                before = now

        def load_x(d):
            return x[pl.ds(base + d, 8, stride=NTH), :]

        def store_tmp(d, v):
            tmp[pl.ds(8 * d, 8), :] = v

        def load_tmp(d):
            return tmp[pl.ds(8 * d, 8), :]

        def store_send(d, v):
            send[pl.ds(base + d, 8, stride=NTH), :] = v

        substep(load_x, store_tmp)
        substep(load_tmp, store_send)


def prepare(cx, cy, nb, ax, ay, chunk):
    first, n = chunk
    width = 128
    lane = lax.broadcasted_iota(jnp.int32, (4, width), 1)
    side = lax.broadcasted_iota(jnp.int32, (4, width), 0)
    shift = jnp.where(side == 0, -1, jnp.where(side == 1, 1, jnp.where(side == 2, -width, width)))

    @pl.loop(0, nb.shape[1] // (8 * width))
    def _(group):
        base = pl.multiple_of(group * (8 * n), 8)
        for j in range(8):
            columns = pl.ds(pl.multiple_of((group * 8 + j) * width, width), width)
            there = (nb[:, columns] == lane + shift + (group * 8 + j) * width).astype(jnp.float32)
            for c, a, low in ((cx, ax, 0), (cy, ay, 2)):
                v = c[pl.ds(first, n), columns]
                a[pl.ds(base + j * n, n), :] = v * jnp.where(v > 0, there[low : low + 1], there[low + 1 : low + 2])


def advect(src, src_at, dst, dst_at, ax, ay, n):
    rows = ax.shape[0]

    def one(row):
        e = src[pl.ds(src_at + row, 8), :]
        south = src[pl.ds(src_at + row - n, 8), :]
        north = src[pl.ds(src_at + row + n, 8), :]
        west, east = pltpu.roll(e, 1, 1), pltpu.roll(e, 127, 1)
        vx, vy = ax[pl.ds(row, 8), :], ay[pl.ds(row, 8), :]
        out = e - jnp.abs(vx) * (e - jnp.where(vx > 0, west, east))
        dst[pl.ds(dst_at + row, 8), :] = out - jnp.abs(vy) * (e - jnp.where(vy > 0, south, north))

    @pl.loop(0, rows // 64)
    def _(step):
        for j in range(8):
            one(pl.multiple_of(step * 64, 8) + 8 * j)


def kernel(x_hbm, r_hbm, cx_hbm, cy_hbm, nb_hbm, out, x, r, cx, cy, nb, tmp, send, *rest):
    nc = len(CHUNKS)
    bufs, (in_sem, own_sem, send_sem, recv_sem) = rest[:-4], rest[-4:]
    recvs, axs, ays, g1s, g2s, backs = (bufs[i * nc : (i + 1) * nc] for i in range(6))
    pts, comp = lax.axis_index("pts"), lax.axis_index("comp")
    me = pts * 8 + comp
    devices = 128
    loads = [
        pltpu.make_async_copy(a, b, in_sem.at[i])
        for i, (a, b) in enumerate(((x_hbm, x), (r_hbm, r), (cx_hbm, cx), (cy_hbm, cy), (nb_hbm, nb)))
    ]
    for c in loads:
        c.start()
    barrier = pltpu.get_barrier_semaphore()

    @pl.loop(1, devices)
    def _(i):
        pl.semaphore_signal(barrier, inc=1, device_id=peer(i, pts, comp), device_id_type=MESH)

    for ref in (*recvs, *g1s, *g2s):
        ref[pl.ds(0, PAD), :] = jnp.zeros((PAD, 128), jnp.float32)
        ref[pl.ds(ref.shape[0] - PAD, PAD), :] = jnp.zeros((PAD, 128), jnp.float32)
    loads[0].wait()
    loads[1].wait()
    refract(x, r, tmp, send)
    pl.semaphore_wait(barrier, devices - 1)

    for j, (first, n) in enumerate(CHUNKS):

        @pl.loop(1, devices)
        def _(i):
            p, c = peer(devices - i, pts, comp)
            to = p * 8 + c
            pltpu.make_async_remote_copy(
                send.at[pl.ds(to * 9 + first, n)],
                recvs[j].at[pl.ds(PAD + me * n, n)],
                send_sem.at[j],
                recv_sem.at[j],
                device_id=(p, c),
                device_id_type=MESH,
            ).start()

        pltpu.make_async_copy(
            send.at[pl.ds(me * 9 + first, n)], recvs[j].at[pl.ds(PAD + me * n, n)], own_sem.at[j]
        ).start()
    for c in loads[2:]:
        c.wait()
    for j, chunk in enumerate(CHUNKS):
        prepare(cx, cy, nb, axs[j], ays[j], chunk)
    for j, (first, n) in enumerate(CHUNKS):
        arrived = recvs[j].at[pl.ds(0, (devices - 1) * n)]
        pltpu.make_async_copy(
            send.at[pl.ds(me * 9 + first, n)], recvs[j].at[pl.ds(PAD + me * n, n)], own_sem.at[j]
        ).wait()
        w = pltpu.make_async_remote_copy(
            arrived, arrived, send_sem.at[j], recv_sem.at[j], device_id=(pts, comp), device_id_type=MESH
        )
        w.wait_recv()
        advect(recvs[j], PAD, g1s[j], PAD, axs[j], ays[j], n)
        advect(g1s[j], PAD, g2s[j], PAD, axs[j], ays[j], n)
        advect(g2s[j], PAD, backs[j], 0, axs[j], ays[j], n)

        @pl.loop(1, devices)
        def _(i):
            p, c = peer(devices - i, pts, comp)
            to = p * 8 + c
            pltpu.make_async_remote_copy(
                backs[j].at[pl.ds(to * n, n)],
                out.at[pl.ds(me * 9 + first, n)],
                send_sem.at[nc + j],
                recv_sem.at[nc + j],
                device_id=(p, c),
                device_id_type=MESH,
            ).start()

        pltpu.make_async_copy(
            backs[j].at[pl.ds(me * n, n)], out.at[pl.ds(me * 9 + first, n)], own_sem.at[nc + j]
        ).start()
    for j, (first, n) in enumerate(CHUNKS):
        pltpu.make_async_copy(
            backs[j].at[pl.ds(me * n, n)], out.at[pl.ds(me * 9 + first, n)], own_sem.at[nc + j]
        ).wait()
        arrived = recvs[j].at[pl.ds(0, (devices - 1) * n)]
        for h in range(2):
            w = pltpu.make_async_remote_copy(
                arrived, arrived, send_sem.at[h * nc + j], recv_sem.at[h * nc + j], device_id=(pts, comp), device_id_type=MESH
            )
            w.wait_send()
            if h == 1:
                w.wait_recv()


def propagate(spectrum, turning, courant_x, courant_y, neighbors):
    f32 = jnp.float32
    any_ = pl.BlockSpec(memory_space=pl.ANY)
    per = [n * 128 for _, n in CHUNKS]
    padded = [pltpu.VMEM((rows + 2 * PAD, 128), f32) for rows in per]
    plain = [pltpu.VMEM((rows, 128), f32) for rows in per]
    nc = len(CHUNKS)
    return pl.pallas_call(
        kernel,
        out_shape=jax.ShapeDtypeStruct((1152, 128), f32),
        in_specs=[any_] * 5,
        out_specs=any_,
        scratch_shapes=[
            pltpu.VMEM((1152, 128), f32),
            pltpu.VMEM((1152, 128), f32),
            pltpu.VMEM((9, 16384), f32),
            pltpu.VMEM((9, 16384), f32),
            pltpu.VMEM((4, 16384), jnp.int32),
            pltpu.VMEM((8 * NTH, 128), f32),
            pltpu.VMEM((1152, 128), f32),
            *padded, *plain, *plain, *padded, *padded, *plain,
            DMA((5,)),
            DMA((2 * nc,)),
            DMA((2 * nc,)),
            DMA((2 * nc,)),
        ],
        name="propagate",
        compiler_params=pltpu.CompilerParams(
            collective_id=1, has_side_effects=True, vmem_limit_bytes=48 * 1024 * 1024
        ),
    )(spectrum, turning, courant_x, courant_y, neighbors)


def body(spectrum, turning, courant_x, courant_y, neighbors, nest_spectra, nest_owner, nest_point, nest_weight):
    point_count = spectrum.shape[1]
    devices = 128
    row_count = nest_spectra.shape[0]
    energy = propagate(spectrum, turning, courant_x, courant_y, neighbors)
    weighted = nest_spectra * nest_weight[:, None]
    owner_ids = nest_owner[:, 0]
    row_index = jnp.arange(row_count, dtype=jnp.int32)
    same_owner = owner_ids[:, None] == owner_ids[None, :]
    earlier = jnp.logical_and(same_owner, row_index[None, :] < row_index[:, None])
    rank_index = jnp.sum(earlier.astype(jnp.int32), axis=1)
    slot_index = owner_ids * CAP + rank_index
    slot_count = devices * CAP
    slot_table = (jnp.arange(slot_count, dtype=jnp.int32)[:, None] == slot_index[None, :]).astype(jnp.float32)
    packed = jnp.dot(slot_table, weighted, precision=lax.Precision.HIGHEST)
    packed_weight = jnp.dot(slot_table, nest_weight, precision=lax.Precision.HIGHEST)
    packed_point = jnp.dot(slot_table, nest_point.astype(jnp.float32), precision=lax.Precision.HIGHEST)
    got_rows, got_weight, got_point = (
        lax.all_to_all(packed, ("pts", "comp"), split_axis=0, concat_axis=0, tiled=True),
        lax.all_to_all(packed_weight, ("pts", "comp"), split_axis=0, concat_axis=0, tiled=True),
        lax.all_to_all(packed_point, ("pts", "comp"), split_axis=0, concat_axis=0, tiled=True),
    )
    point_table = (
        got_point.astype(jnp.int32)[:, None] == jnp.arange(point_count, dtype=jnp.int32)[None, :]
    ).astype(jnp.float32)
    added_energy = lax.dot_general(got_rows, point_table, (((0,), (0,)), ((), ())), precision=lax.Precision.HIGHEST)
    total_weight = jnp.dot(got_weight, point_table, precision=lax.Precision.HIGHEST)
    return (energy + added_energy) / (1.0 + total_weight)[None, :]


def solution(mesh):
    placed = (
        P(None, ("pts", "comp")),
        P(None, ("pts", "comp")),
        P(("pts", "comp"), None),
        P(("pts", "comp"), None),
        P(),
        P(("pts", "comp"), None),
        P(("pts", "comp"), None),
        P(("pts", "comp")),
        P(("pts", "comp")),
    )
    return jax.shard_map(body, mesh=mesh, in_specs=placed, out_specs=P(None, ("pts", "comp")), check_vma=False)
```

time: 158 us -> 109 us (0.69)
  Pallas kernels: 0 us -> 53.7 us
  waiting for transfers between devices: 64.9 us -> 13.3 us
  local copies, waits for them, and re-layouts: 31.4 us -> 8.34 us
  starting transfers between devices: 36.7 us -> 22.3 us
  other arithmetic: 15.8 us -> 3.42 us
    pallas_call x0 -> x1, Pallas kernels: none -> 53.7 us  [propagate(): pl.pallas_call(kernel, out_shape=jax.ShapeDtypeStruct((1152, 128), f32),...]
    all_to_all x2 -> x0, waiting for transfers between devices: 31.1 us -> none  [the longest x1 16 us: body(): lax.all_to_all(blocks, ('pts', 'comp'), split_axis=0, concat_axis=2, tile...]
    all_to_all x1, waiting for transfers between devices: 28.7 us -> 0.01 us  [body(): lax.all_to_all(packed, ('pts', 'comp'), split_axis=0, concat_axis=0, tile...]
    all_to_all x2 -> x0, starting transfers between devices: 16.5 us -> none  [the longest x1 11.5 us: body(): lax.all_to_all(blocks, ('pts', 'comp'), split_axis=0, concat_axis=2, tile...]
    add x6 -> x0, other arithmetic: 7.9 us -> none  [the longest x2 4.68 us: refract(): return energy - fluxes + jnp.roll(fluxes, 1, axis=1)]
    concatenate x4 -> x0, local copies, waits for them, and re-layouts: 7.62 us -> none  [the longest x2 4.38 us: refract(): upstream = jnp.roll(energy, -1, axis=1)]
    all_to_all x1, waiting for transfers between devices: 0.32 us -> 7.84 us  [body(): lax.all_to_all(packed_point, ('pts', 'comp'), split_axis=0, concat_axis=0...]
    slice x19 -> x0, local copies, waits for them, and re-layouts: 6.69 us -> none  [the longest x12 4.87 us: pick_upwind(): after = jnp.roll(energy, -stride, axis=1)]
  transfers between devices with their start and end apart: 5 -> 3, of which waited for: 5 -> 2; matrix products, arithmetic and copies ran while one was open for 13% -> 5% of each run, Pallas kernels for 0% -> 50%
where the time goes in v1:
time: 109 us; the launch traced here: 108 us
  Pallas kernels  53.7 us (49%)
  starting transfers between devices  22.3 us (20%)
  waiting for transfers between devices  13.3 us (12%)
  local copies, waits for them, and re-layouts  8.34 us (8%)
  matrix products  7.18 us (7%)
  other arithmetic  3.42 us (3%)
    pallas_call x1, Pallas kernels, propagate(): pl.pallas_call(kernel, out_shape=jax.ShapeDtypeStruct((1152, 128), f32),...  53.7 us
    all_to_all x1, starting transfers between devices, body(): lax.all_to_all(packed_point, ('pts', 'comp'), split_axis=0, concat_axis=0...  11.5 us
    all_to_all x1, waiting for transfers between devices, body(): lax.all_to_all(packed_point, ('pts', 'comp'), split_axis=0, concat_axis=0...  7.84 us
    all_to_all x1, starting transfers between devices, body(): lax.all_to_all(packed, ('pts', 'comp'), split_axis=0, concat_axis=0, tile...  5.56 us
    all_to_all x1, waiting for transfers between devices, body(): lax.all_to_all(packed_weight, ('pts', 'comp'), split_axis=0, concat_axis=...  5.45 us
    all_to_all x1, starting transfers between devices, body(): lax.all_to_all(packed_weight, ('pts', 'comp'), split_axis=0, concat_axis=...  5.26 us
    all_to_all x2, local copies, waits for them, and re-layouts, body(): lax.all_to_all(packed, ('pts', 'comp'), split_axis=0, concat_axis=0, tile...  4.42 us
    dot_general x1, matrix products, body(): lax.dot_general(got_rows, point_table, (((0,), (0,)), ((), ())), precisio...  2.92 us
  transfers between devices with their start and end apart: 3, of which 2 were waited for; matrix products, arithmetic and copies ran while one was open for 5% of the time, Pallas kernels for 50%

profile of v1, /device:TPU:1, one launch (start us, length us, event | category | flops | bytes accessed | tf_op | source)
XLA Modules:
  0.0 108.4 jit_solution(4172297917756811658)
XLA Ops:
  0.0 0.9 convert_reduce_fusion.1
  0.9 0.7 multiply_add_fusion
  1.6 0.9 fusion.5
  2.5 0.7 all_to_all.25
  3.2 11.5 %all-to-all-start.1 = ((f32[128,4,1]{1,2,0:T(1,128)}), f32[128,4,1]{1,2,0:T(1,128)S(1)}, u32[]{:S(2)}, u32[]{:S(2)}) async-start(f32[128,4,1]{1,2,0:T(1,128)} %bitcast.3), calls=%async_computation.1 | async-start | bytes 131072 | tf_op jit(solution)/shard_map/all_to_all | solution.py:244
  14.7 0.9 fusion.4
  15.6 0.8 all_to_all.27
  16.4 7.8 %all-to-all-done.1 = f32[128,4,1]{1,2,0:T(1,128)S(1)} async-done(((f32[128,4,1]{1,2,0:T(1,128)}), f32[128,4,1]{1,2,0:T(1,128)S(1)}, u32[]{:S(2)}, u32[]{:S(2)}) %all-to-all-start.1) | async-done | bytes 2080 | tf_op jit(solution)/shard_map/all_to_all | solution.py:244
  24.2 0.0 copy-start.5
  24.2 0.6 copy-done.5
  24.8 5.3 %all-to-all-start.2 = ((f32[128,4,1]{1,2,0:T(1,128)}), f32[128,4,1]{1,2,0:T(1,128)}, u32[]{:S(2)}, u32[]{:S(2)}) async-start(f32[128,4,1]{1,2,0:T(1,128)} %bitcast.6), calls=%async_computation.2 | async-start | bytes 131072 | tf_op jit(solution)/shard_map/all_to_all | solution.py:243
  30.1 2.2 %fusion.2 = f32[512,1152]{1,0:T(8,128)S(1)} fusion(f32[104,1152]{1,0:T(8,128)} %param.14, f32[104]{0:T(128)} %param.17, s32[104]{0:T(128)S(1)} %multiply_add_fusion), kind=kOutput, calls=%fused_computation.4 | convolution fusion | flops 736273408 | bytes 2839360 | tf_op jit(solution)/shard_map/dot_general | solution.py:238
  32.3 1.8 %all_to_all.22 = f32[128,4,1152]{2,1,0:T(4,128)} reshape(f32[512,1152]{1,0:T(8,128)S(1)} %fusion.2) | data formatting | bytes 4718592 | tf_op jit(solution)/shard_map/all_to_all | solution.py:242
  34.1 0.0 copy-start
  34.1 0.0 copy-start.1
  34.1 0.0 copy-start.2
  34.1 0.0 copy-start.4
  34.1 5.4 %all-to-all-done.2 = f32[128,4,1]{1,2,0:T(1,128)} async-done(((f32[128,4,1]{1,2,0:T(1,128)}), f32[128,4,1]{1,2,0:T(1,128)}, u32[]{:S(2)}, u32[]{:S(2)}) %all-to-all-start.2) | async-done | bytes 2080 | tf_op jit(solution)/shard_map/all_to_all | solution.py:243
  39.5 5.6 %all-to-all-start = ((f32[128,4,1152]{2,1,0:T(4,128)}), f32[128,4,1152]{2,1,0:T(4,128)}, u32[]{:S(2)}, u32[]{:S(2)}) async-start(f32[128,4,1152]{2,1,0:T(4,128)} %all_to_all.22), calls=%async_computation | async-start | bytes 4718592 | tf_op jit(solution)/shard_map/all_to_all | solution.py:242
  45.1 0.0 copy-done
  45.1 0.0 copy-done.1
  45.1 0.0 copy-done.2
  45.1 0.0 copy-done.4
  45.1 0.0 copy-start.3
  45.1 1.1 copy-done.3
  46.2 0.0 copy-start.6
  46.2 53.7 %propagate.1 = f32[1152,128]{1,0:T(8,128)S(1)} custom-call(f32[1152,128]{1,0:T(8,128)S(1)} %copy-done.2, f32[1152,128]{1,0:T(8,128)S(1)} %copy-done.3, f32[9,16384]{1,0:T(8,128)S(1)} %copy-done, f32[9,16384]{1,0:T(8,128)S(1)} %copy-done.1, s32[4,16384]{1,0:T(4,128)S(1)} %copy-done.4), custom_call_target="tpu_custom_call" | custom-call | tf_op jit(solution)/shard_map/propagate/pallas_call | solution.py:198
  99.9 0.0 copy-done.6
  99.9 0.2 convert_reduce_fusion
  100.1 0.1 convert_element_type.21
  100.2 0.5 broadcast.12
  100.8 1.6 %reduce.7 = f32[128,4]{1,0:T(8,128)S(1)} reduce(f32[128,4,1]{1,2,0:T(1,128)} %all-to-all-done.2, f32[]{:T(128)} %broadcast.12), dimensions={2}, to_apply=%all_to_all.28.reduce_sub_computation.3 | reduce | bytes 4100 | tf_op jit(solution)/shard_map/all_to_all | solution.py:243
  102.4 0.1 reshape.27
  102.5 0.3 fusion.1
  102.8 0.0 all-to-all-done
  102.8 2.7 %all_to_all.24 = f32[512,1152]{1,0:T(8,128)S(1)} reshape(f32[128,4,1152]{2,1,0:T(4,128)} %all-to-all-done) | data formatting | bytes 4718592 | tf_op jit(solution)/shard_map/all_to_all | solution.py:242
  105.5 2.9 %fusion = f32[1152,128]{1,0:T(8,128)} fusion(f32[1152,128]{1,0:T(8,128)S(1)} %propagate.1, f32[512,1152]{1,0:T(8,128)S(1)} %all_to_all.24, f32[128]{0:T(128)S(1)} %fusion.1, s32[512]{0:T(512)S(1)} %convert_element_type.21), kind=kOutput, calls=%fused_computation.1 | convolution fusion | flops 906330112 | bytes 3541504 | tf_op jit(solution)/shard_map/dot_general | solution.py:249
Async XLA Ops:
  3.2 21.0 %all-to-all-start.1 = ((f32[128,4,1]{1,2,0:T(1,128)}), f32[128,4,1]{1,2,0:T(1,128)S(1)}, u32[]{:S(2)}, u32[]{:S(2)}) async-start(f32[128,4,1]{1,2,0:T(1,128)} %bitcast.3), calls=%async_computation.1 | async-start | bytes 131072 | tf_op jit(solution)/shard_map/all_to_all | solution.py:244
  24.2 0.6 copy-start.5
  24.8 14.7 %all-to-all-start.2 = ((f32[128,4,1]{1,2,0:T(1,128)}), f32[128,4,1]{1,2,0:T(1,128)}, u32[]{:S(2)}, u32[]{:S(2)}) async-start(f32[128,4,1]{1,2,0:T(1,128)} %bitcast.6), calls=%async_computation.2 | async-start | bytes 131072 | tf_op jit(solution)/shard_map/all_to_all | solution.py:243
  34.1 11.0 %copy-start = (f32[9,16384]{1,0:T(8,128)S(1)}, f32[9,16384]{1,0:T(8,128)}, u32[]{:S(2)}) copy-start(f32[9,16384]{1,0:T(8,128)} %cx_hbm.1) | copy-start | bytes 1769476
  34.1 11.0 %copy-start.1 = (f32[9,16384]{1,0:T(8,128)S(1)}, f32[9,16384]{1,0:T(8,128)}, u32[]{:S(2)}) copy-start(f32[9,16384]{1,0:T(8,128)} %cy_hbm.1) | copy-start | bytes 1769476
  34.1 11.0 %copy-start.2 = (f32[1152,128]{1,0:T(8,128)S(1)}, f32[1152,128]{1,0:T(8,128)}, u32[]{:S(2)}) copy-start(f32[1152,128]{1,0:T(8,128)} %x_hbm.1) | copy-start | bytes 1769476
  34.1 11.0 %copy-start.4 = (s32[4,16384]{1,0:T(4,128)S(1)}, s32[4,16384]{1,0:T(4,128)}, u32[]{:S(2)}) copy-start(s32[4,16384]{1,0:T(4,128)} %nb_hbm.1) | copy-start | bytes 786436
  39.5 63.3 %all-to-all-start = ((f32[128,4,1152]{2,1,0:T(4,128)}), f32[128,4,1152]{2,1,0:T(4,128)}, u32[]{:S(2)}, u32[]{:S(2)}) async-start(f32[128,4,1152]{2,1,0:T(4,128)} %all_to_all.22), calls=%async_computation | async-start | bytes 4718592 | tf_op jit(solution)/shard_map/all_to_all | solution.py:242
  45.1 1.1 copy-start.3
  46.2 53.7 %copy-start.6 = (f32[128,4,1]{1,2,0:T(1,128)S(1)}, f32[128,4,1]{1,2,0:T(1,128)}, u32[]{:S(2)}) copy-start(f32[128,4,1]{1,2,0:T(1,128)} %copy-done.5) | copy-start | bytes 6148

commit v2 on v0

v2 whole, which is shorter than its diff:
```python
import functools

import jax
import jax.numpy as jnp
from jax import lax
from jax.experimental import pallas as pl
from jax.experimental.pallas import tpu as pltpu
from jax.sharding import PartitionSpec as P

MESH = pl.DeviceIdType.MESH
DMA = pltpu.SemaphoreType.DMA
F32 = jnp.float32
BF16 = jnp.bfloat16
NTH = 36
DEVICES = 128
WIDTH = 128
COMPS = 1152
OWN = 9
PAD = 16
STEPS = 136
UNROLL = 7
PARTS = ((0, 4, 5, (3, 1)), (4, 3, 1, (5, 3)), (7, 3, 3, (5, 1)))


def at(device):
    return dict(device_id=(device // 8, device % 8), device_id_type=MESH)


def digit(index, bit):
    return (index >> bit) & 3


def each_peer(body):
    def some(j, carry):
        for q in range(UNROLL):
            body(DEVICES - 1 - (j * UNROLL + q))
        return carry

    whole = (DEVICES - 1) // UNROLL
    lax.fori_loop(0, whole, some, 0)
    for i in range(DEVICES - 1 - whole * UNROLL, 0, -1):
        body(i)


def far_first(i):
    high, low = i & 0b1010100, i & 0b0101010
    return (low << 1) | ((high >> 1) ^ low) | (i & 1)


def refract(x, r, tmp, send):
    @pl.loop(0, x.shape[0] // (8 * NTH))
    def _(group):
        base = pl.multiple_of(group * (8 * NTH), 8)

        def substep(load, store):
            def flux(d):
                rate = r[pl.ds(base + d, 8, stride=NTH), :]
                return jnp.maximum(rate, 0.0) * load(d) + jnp.minimum(rate, 0.0) * load((d + 1) % NTH)

            before = flux(NTH - 1)
            for d in range(NTH):
                now = flux(d)
                store(d, load(d) - now + before)
                before = now

        def load_x(d):
            return x[pl.ds(base + d, 8, stride=NTH), :]

        def store_tmp(d, v):
            tmp[pl.ds(8 * d, 8), :] = v

        def load_tmp(d):
            return tmp[pl.ds(8 * d, 8), :]

        def store_send(d, v):
            send[pl.ds(base + d, 8, stride=NTH), :] = v

        substep(load_x, store_tmp)
        substep(load_tmp, store_send)


def local_sums(spectra, owner, point, weight, sums):
    rows = spectra.shape[0]
    w = weight[...]
    diagonal = lax.broadcasted_iota(jnp.int32, (rows, rows), 0) == lax.broadcasted_iota(jnp.int32, (rows, rows), 1)
    w_column = jnp.sum(jnp.where(diagonal, w, 0.0), axis=1, keepdims=True)
    o = owner[...]
    end = (point[...] > 0).astype(jnp.int32)
    place = lax.broadcasted_iota(jnp.int32, (256, rows), 0)
    for (first, tiles, bit, (b1, b2)), out in zip(PARTS, sums):
        target = (o & 1) * 128 + digit(o, bit) * 32 + digit(o, b1) * 8 + digit(o, b2) * 2 + end
        table = (place == target).astype(F32).astype(BF16)
        for t in range(tiles):
            if first + t < COMPS // WIDTH:
                v = spectra[:, (first + t) * WIDTH : (first + t + 1) * WIDTH] * w_column
            else:
                v = jnp.broadcast_to(w_column, (rows, WIDTH))
            high = v.astype(BF16)
            low = (v - high.astype(F32)).astype(BF16)
            out[:, t * WIDTH : (t + 1) * WIDTH] = jnp.dot(table, high, preferred_element_type=F32) + jnp.dot(
                table, low, preferred_element_type=F32
            )


def prepare(cx, cy, nb, axa, aya, axb, ayb):
    lane = lax.broadcasted_iota(jnp.int32, (4, WIDTH), 1)
    side = lax.broadcasted_iota(jnp.int32, (4, WIDTH), 0)
    shift = lane + jnp.where(side == 0, -1, jnp.where(side == 1, 1, jnp.where(side == 2, -WIDTH, WIDTH)))
    for a in (axa, aya):
        a[pl.ds(0, 16), :] = jnp.zeros((16, WIDTH), F32)
        a[pl.ds(16 + 8 * DEVICES, 8 * (STEPS - DEVICES)), :] = jnp.zeros((8 * (STEPS - DEVICES), WIDTH), F32)

    @pl.loop(0, DEVICES // 8)
    def _(group):
        for j in range(8):
            s = group * 8 + j
            columns = pl.ds(pl.multiple_of(s * WIDTH, WIDTH), WIDTH)
            there = (nb[:, columns] == shift + s * WIDTH).astype(F32)
            for c, a, b, low in ((cx, axa, axb, 0), (cy, aya, ayb, 2)):
                up, down = there[low : low + 1], there[low + 1 : low + 2]
                v = c[pl.ds(0, 8), columns]
                a[pl.ds(pl.multiple_of((s + 2) * 8, 8), 8), :] = v * jnp.where(v > 0, up, down)
                v = c[pl.ds(8, 1), columns]
                b[pl.ds(pl.multiple_of(group * 8, 8) + j, 1), :] = v * jnp.where(v > 0, up, down)


def upwind(e, south, north, vx, vy):
    west, east = pltpu.roll(e, 1, 1), pltpu.roll(e, WIDTH - 1, 1)
    out = e - jnp.abs(vx) * (e - jnp.where(vx > 0, west, east))
    return out - jnp.abs(vy) * (e - jnp.where(vy > 0, south, north))


def advect(recv, back, axa, aya, axb, ayb):
    zero = jnp.zeros((8, WIDTH), F32)

    def steps(group, carry):
        e0m, e0, e1m, e1, e2m, e2, x1, y1, x2, y2 = carry
        base = pl.multiple_of(group * 72, 8)
        courant = pl.multiple_of(group * 64, 8)
        for j in range(8):
            e0p = recv[pl.ds(base + (PAD + 9 * (j + 1)), 8), :]
            x0 = axa[pl.ds(courant + 8 * (j + 2), 8), :]
            y0 = aya[pl.ds(courant + 8 * (j + 2), 8), :]
            e1p = upwind(e0, e0m, e0p, x0, y0)
            e2p = upwind(e1, e1m, e1p, x1, y1)
            back[pl.ds(base + (24 + 9 * (j - 2)), 8), :] = upwind(e2, e2m, e2p, x2, y2)
            e0m, e0, e1m, e1, e2m, e2 = e0, e0p, e1, e1p, e2, e2p
            x2, y2, x1, y1 = x1, y1, x0, y0
        return e0m, e0, e1m, e1, e2m, e2, x1, y1, x2, y2

    lax.fori_loop(0, STEPS // 8, steps, (zero, recv[pl.ds(PAD, 8), :]) + (zero,) * 8)
    groups = DEVICES // 8
    e = [recv[pl.ds(PAD + 8 + 72 * g, 8, stride=OWN), :] for g in range(groups)]
    row = lax.broadcasted_iota(jnp.int32, (8, WIDTH), 0)
    for _ in range(3):
        up = [pltpu.roll(v, 1, 0) for v in e]
        down = [pltpu.roll(v, 7, 0) for v in e]
        e = [
            upwind(
                e[g],
                jnp.where(row == 0, up[g - 1], up[g]),
                jnp.where(row == 7, down[(g + 1) % groups], down[g]),
                axb[pl.ds(8 * g, 8), :],
                ayb[pl.ds(8 * g, 8), :],
            )
            for g in range(groups)
        ]
    for g in range(groups):
        back[pl.ds(24 + 8 + 72 * g, 8, stride=OWN), :] = e[g]


def kernel(
    x_hbm, r_hbm, cx_hbm, cy_hbm, nb_hbm, ns_hbm, owner_hbm, point_hbm, weight_hbm, out, added_hbm, scale_hbm, *scratch
):
    x, r, cx, cy, nb, ns, owner, point, weight = scratch[:9]
    tmp, send, recv, back, axa, aya, axb, ayb, added, scale = scratch[9:19]
    sums, pair, chip, first_in, second_out, second_in = (scratch[19 + 3 * i : 22 + 3 * i] for i in range(6))
    in_sem, own_sem, send_sem, recv_sem, result_sem, part_send, part_recv = scratch[37:]
    me = lax.axis_index("pts") * 8 + lax.axis_index("comp")
    loads = [
        pltpu.make_async_copy(a, b, in_sem.at[i])
        for i, (a, b) in enumerate(
            (
                (x_hbm, x),
                (r_hbm, r),
                (ns_hbm, ns),
                (owner_hbm, owner),
                (point_hbm, point),
                (weight_hbm, weight),
                (cx_hbm, cx),
                (cy_hbm, cy),
                (nb_hbm, nb),
            )
        )
    ]
    for c in loads:
        c.start()
    barrier = pltpu.get_barrier_semaphore()
    each_peer(lambda i: pl.semaphore_signal(barrier, inc=1, **at(me ^ i)))

    recv[pl.ds(0, PAD), :] = jnp.zeros((PAD, WIDTH), F32)
    tail = recv.shape[0] - PAD - COMPS
    recv[pl.ds(PAD + COMPS, tail), :] = jnp.zeros((tail, WIDTH), F32)
    loads[0].wait()
    loads[1].wait()
    refract(x, r, tmp, send)
    for c in loads[2:6]:
        c.wait()
    local_sums(ns, owner, point, weight, sums)
    pl.semaphore_wait(barrier, DEVICES - 1)

    def over(stage, p, ref, source, target, device):
        return pltpu.make_async_remote_copy(source, target, part_send.at[stage, p], part_recv.at[stage, p], **at(device))

    def wait_part(stage, p, ref):
        w = over(stage, p, ref, ref, ref, me)
        w.wait_recv()
        w.wait_send()

    for p in range(3):
        other = pl.ds(pl.multiple_of((1 - me % 2) * 128, 128), 128)
        over(0, p, None, sums[p].at[other], pair[p], me ^ 1).start()

    def transpose(stage, source, target, source_at, target_at):
        def start(i):
            to = me ^ far_first(i)
            pltpu.make_async_remote_copy(
                source.at[pl.ds(source_at + to * OWN, OWN)],
                target.at[pl.ds(target_at + me * OWN, OWN)],
                send_sem.at[stage],
                recv_sem.at[stage],
                **at(to),
            ).start()

        each_peer(start)
        own = pltpu.make_async_copy(
            source.at[pl.ds(source_at + me * OWN, OWN)], target.at[pl.ds(target_at + me * OWN, OWN)], own_sem.at[stage]
        )
        own.start()
        rest = recv.at[pl.ds(0, (DEVICES - 1) * OWN)]
        return own, pltpu.make_async_remote_copy(rest, rest, send_sem.at[stage], recv_sem.at[stage], **at(me))

    own, moved = transpose(0, send, recv, 0, PAD)

    for p, (first, tiles, bit, _) in enumerate(PARTS):
        wait_part(0, p, pair[p])
        mine = pl.ds(pl.multiple_of((me % 2) * 128, 128), 128)
        chip[p][...] = sums[p][mine, :] + pair[p][...]
        for d in range(1, 4):
            to = me ^ (d << bit)
            block = pl.ds(pl.multiple_of(digit(to, bit) * 32, 32), 32)
            over(1, p, None, chip[p].at[block], first_in[p].at[pl.ds((d - 1) * 32, 32)], to).start()

    for c in loads[6:]:
        c.wait()
    prepare(cx, cy, nb, axa, aya, axb, ayb)
    own.wait()
    moved.wait_recv()
    advect(recv, back, axa, aya, axb, ayb)
    own2, moved2 = transpose(1, back, out, 24, 0)

    for p, (first, tiles, bit, (b1, b2)) in enumerate(PARTS):
        wait_part(1, p, first_in[p])
        block = pl.ds(pl.multiple_of(digit(me, bit) * 32, 32), 32)
        for t in range(4):
            if t < tiles:
                lanes = slice(t * WIDTH, (t + 1) * WIDTH)
                v = chip[p][block, lanes]
                for d in range(3):
                    v = v + first_in[p][d * 32 : (d + 1) * 32, lanes]
            else:
                v = jnp.zeros((32, WIDTH), F32)
            second_out[p][pl.ds(t, 32, stride=4), :] = v

        @pl.loop(1, 16)
        def _(q):
            to = me ^ (((q >> 2) << b1) | ((q & 3) << b2))
            block = digit(to, b1) * 4 + digit(to, b2)
            over(
                2,
                p,
                None,
                second_out[p].at[pl.ds(pl.multiple_of(block * 8, 8), 8)],
                second_in[p].at[pl.ds(pl.multiple_of(q * 8, 8), 8)],
                to,
            ).start()

    lane = lax.broadcasted_iota(jnp.int32, (WIDTH, WIDTH), 1)
    for p, (first, tiles, bit, (b1, b2)) in enumerate(PARTS):
        wait_part(2, p, second_in[p].at[pl.ds(8, 120)])
        block = digit(me, b1) * 4 + digit(me, b2)
        v = second_out[p][pl.ds(pl.multiple_of(block * 8, 8), 8), :]
        for q in range(1, 16):
            v = v + second_in[p][pl.ds(8 * q, 8), :]
        columns = v.T
        for t in range(tiles):
            if first + t < COMPS // WIDTH:
                added[pl.ds((first + t) * WIDTH, WIDTH), :] = jnp.where(
                    lane == 0, columns[:, t : t + 1], jnp.where(lane == WIDTH - 1, columns[:, 4 + t : 5 + t], 0.0)
                )
            else:
                one = lax.broadcasted_iota(jnp.int32, (8, WIDTH), 1)
                total = jnp.where(one == 0, v[t : t + 1], jnp.where(one == WIDTH - 1, v[4 + t : 5 + t], 0.0))
                scale[...] = 1.0 / (1.0 + total)
    results = [
        pltpu.make_async_copy(added, added_hbm, result_sem.at[0]),
        pltpu.make_async_copy(scale, scale_hbm, result_sem.at[1]),
    ]
    for c in results:
        c.start()
    moved.wait_send()
    for c in results:
        c.wait()
    own2.wait()
    moved2.wait_send()
    moved2.wait_recv()


def timestep(*arrays):
    whole = [pltpu.VMEM(a.shape, a.dtype) for a in arrays]
    anywhere = pl.BlockSpec(memory_space=pl.ANY)

    def rows(n):
        return pltpu.VMEM((n, WIDTH), F32)

    def parts(n):
        return [pltpu.VMEM((n, tiles * WIDTH), F32) for _, tiles, _, _ in PARTS]

    return pl.pallas_call(
        kernel,
        out_shape=(
            jax.ShapeDtypeStruct((COMPS, WIDTH), F32),
            jax.ShapeDtypeStruct((COMPS, WIDTH), F32),
            jax.ShapeDtypeStruct((8, WIDTH), F32),
        ),
        in_specs=[anywhere] * 9,
        out_specs=(anywhere,) * 3,
        scratch_shapes=[
            *whole,
            rows(8 * NTH),
            rows(COMPS),
            rows(PAD + OWN * (STEPS + 2)),
            rows(24 + OWN * STEPS),
            rows(8 * (STEPS + 2)),
            rows(8 * (STEPS + 2)),
            rows(DEVICES),
            rows(DEVICES),
            rows(COMPS),
            rows(8),
            *parts(256),
            *parts(128),
            *parts(128),
            *parts(96),
            *[rows(128) for _ in PARTS],
            *[rows(128) for _ in PARTS],
            DMA((9,)),
            DMA((2,)),
            DMA((2,)),
            DMA((2,)),
            DMA((2,)),
            DMA((3, 3)),
            DMA((3, 3)),
        ],
        name="timestep",
        compiler_params=pltpu.CompilerParams(
            collective_id=1, has_side_effects=True, vmem_limit_bytes=48 * 1024 * 1024
        ),
    )(*arrays)


def body(spectrum, turning, courant_x, courant_y, neighbors, nest_spectra, nest_owner, nest_point, nest_weight):
    rows = nest_spectra.shape[0]
    energy, added, scale = timestep(
        spectrum,
        turning,
        courant_x,
        courant_y,
        neighbors,
        nest_spectra,
        nest_owner.reshape(1, rows),
        nest_point.reshape(1, rows),
        nest_weight.reshape(1, rows),
    )
    return (energy + added) * scale[0:1, :]


def solution(mesh):
    placed = (
        P(None, ("pts", "comp")),
        P(None, ("pts", "comp")),
        P(("pts", "comp"), None),
        P(("pts", "comp"), None),
        P(),
        P(("pts", "comp"), None),
        P(("pts", "comp"), None),
        P(("pts", "comp")),
        P(("pts", "comp")),
    )
    return jax.shard_map(body, mesh=mesh, in_specs=placed, out_specs=P(None, ("pts", "comp")), check_vma=False)
```

time: 158 us -> 47.6 us (0.30)
  waiting for transfers between devices: 64.9 us -> 0 us
  Pallas kernels: 0 us -> 39.1 us
  starting transfers between devices: 36.7 us -> 0 us
  local copies, waits for them, and re-layouts: 31.4 us -> 7.23 us
  other arithmetic: 15.8 us -> 0.88 us
  matrix products: 7.53 us -> 0 us
    all_to_all x5 -> x0, waiting for transfers between devices: 64.9 us -> none  [the longest x1 28.7 us: body(): lax.all_to_all(packed, ('pts', 'comp'), split_axis=0, concat_axis=0, tile...]
    pallas_call x0 -> x1, Pallas kernels: none -> 39.1 us  [timestep(): pl.pallas_call(kernel, out_shape=(jax.ShapeDtypeStruct((COMPS, WIDTH), F3...]
    all_to_all x5 -> x0, starting transfers between devices: 36.7 us -> none  [the longest x1 11.5 us: body(): lax.all_to_all(blocks, ('pts', 'comp'), split_axis=0, concat_axis=2, tile...]
    add x7 -> x0, other arithmetic: 7.91 us -> none  [the longest x2 4.68 us: refract(): return energy - fluxes + jnp.roll(fluxes, 1, axis=1)]
    concatenate x4 -> x0, local copies, waits for them, and re-layouts: 7.62 us -> none  [the longest x2 4.38 us: refract(): upstream = jnp.roll(energy, -1, axis=1)]
    dot_general x5 -> x0, matrix products: 7.53 us -> none  [the longest x1 4.58 us: body(): lax.dot_general(got_rows, point_table, (((0,), (0,)), ((), ())), precisio...]
    slice x19 -> x0, local copies, waits for them, and re-layouts: 6.69 us -> none  [the longest x12 4.87 us: pick_upwind(): after = jnp.roll(energy, -stride, axis=1)]
    all_to_all x7 -> x0, local copies, waits for them, and re-layouts: 5.91 us -> none  [the longest x2 3.61 us: body(): lax.all_to_all(packed, ('pts', 'comp'), split_axis=0, concat_axis=0, tile...]
  transfers between devices with their start and end apart: 5 -> 0, of which waited for: 5 -> 0; matrix products, arithmetic and copies ran while one was open for 13% -> 0% of each run, Pallas kernels for 0% -> 0%
where the time goes in v2:
time: 47.6 us; the launch traced here: 47.3 us
  Pallas kernels  39.1 us (82%)
  local copies, waits for them, and re-layouts  7.23 us (15%)
  other arithmetic  0.88 us (2%)
    pallas_call x1, Pallas kernels, timestep(): pl.pallas_call(kernel, out_shape=(jax.ShapeDtypeStruct((COMPS, WIDTH), F3...  39.1 us
    unnamed x18, local copies, waits for them, and re-layouts  7.23 us

profile of v2, /device:TPU:1, one launch (start us, length us, event | category | flops | bytes accessed | tf_op | source)
XLA Modules:
  0.0 47.3 jit_solution(6928130439269019214)
XLA Ops:
  0.0 0.0 copy-start.6
  0.0 0.0 copy-start.7
  0.0 0.0 copy-start.8
  0.0 0.6 %copy-done.6 = s32[104,1]{0,1:T(1,128)S(1)} copy-done((s32[104,1]{0,1:T(1,128)S(1)}, s32[104,1]{0,1:T(1,128)}, u32[]{:S(2)}) %copy-start.6) | copy-done | bytes 440
  0.7 0.0 copy-done.7
  0.7 0.0 copy-done.8
  0.7 0.0 copy-start
  0.7 1.2 %copy-done = f32[9,16384]{1,0:T(8,128)S(1)} copy-done((f32[9,16384]{1,0:T(8,128)S(1)}, f32[9,16384]{1,0:T(8,128)}, u32[]{:S(2)}) %copy-start) | copy-done | bytes 589848
  1.9 0.0 copy-start.1
  1.9 1.2 %copy-done.1 = f32[9,16384]{1,0:T(8,128)S(1)} copy-done((f32[9,16384]{1,0:T(8,128)S(1)}, f32[9,16384]{1,0:T(8,128)}, u32[]{:S(2)}) %copy-start.1) | copy-done | bytes 589848
  3.1 0.0 copy-start.2
  3.1 1.1 %copy-done.2 = f32[1152,128]{1,0:T(8,128)S(1)} copy-done((f32[1152,128]{1,0:T(8,128)S(1)}, f32[1152,128]{1,0:T(8,128)}, u32[]{:S(2)}) %copy-start.2) | copy-done | bytes 589848
  4.2 0.0 copy-start.3
  4.2 1.1 %copy-done.3 = f32[1152,128]{1,0:T(8,128)S(1)} copy-done((f32[1152,128]{1,0:T(8,128)S(1)}, f32[1152,128]{1,0:T(8,128)}, u32[]{:S(2)}) %copy-start.3) | copy-done | bytes 589848
  5.3 0.0 copy-start.4
  5.3 1.0 %copy-done.4 = f32[104,1152]{1,0:T(8,128)S(1)} copy-done((f32[104,1152]{1,0:T(8,128)S(1)}, f32[104,1152]{1,0:T(8,128)}, u32[]{:S(2)}) %copy-start.4) | copy-done | bytes 479256
  6.3 0.0 copy-start.5
  6.3 0.9 %copy-done.5 = s32[4,16384]{1,0:T(4,128)S(1)} copy-done((s32[4,16384]{1,0:T(4,128)S(1)}, s32[4,16384]{1,0:T(4,128)}, u32[]{:S(2)}) %copy-start.5) | copy-done | bytes 262168
  7.2 39.1 %timestep.1 = (f32[1152,128]{1,0:T(8,128)S(1)}, f32[1152,128]{1,0:T(8,128)S(1)}, f32[8,128]{1,0:T(8,128)S(1)}) custom-call(f32[1152,128]{1,0:T(8,128)S(1)} %copy-done.2, f32[1152,128]{1,0:T(8,128)S(1)} %copy-done.3, f32[9,16384]{1,0:T(8,128)S(1)} %copy-done, f32[9,16384]{1,0:T(8,128)S(1)} %copy-done.1, s32[4,16384]{1,0:T(4,128)S(1)} %copy-done.5, ...), custom_call_target="tpu_custom_call" | custom-call | tf_op jit(solution)/shard_map/timestep/pallas_call | solution.py:329
  46.4 0.9 %add_multiply_fusion = f32[1152,128]{1,0:T(8,128)} fusion(f32[1152,128]{1,0:T(8,128)S(1)} %get-tuple-element.8, f32[1152,128]{1,0:T(8,128)S(1)} %get-tuple-element.9, f32[128]{0:T(128)S(1)} %slice_bitcast_fusion), kind=kLoop, calls=%fused_computation | loop fusion | flops 294912 | bytes 1769984 | tf_op jit(solution)/shard_map/mul | solution.py:384
  (1 shorter events, 0.0 us)
Async XLA Ops:
  0.0 0.7 %copy-start.6 = (s32[104,1]{0,1:T(1,128)S(1)}, s32[104,1]{0,1:T(1,128)}, u32[]{:S(2)}) copy-start(s32[104,1]{0,1:T(1,128)} %param.15) | copy-start | bytes 1252
  0.0 0.7 %copy-start.7 = (s32[104]{0:T(128)S(1)}, s32[104]{0:T(128)}, u32[]{:S(2)}) copy-start(s32[104]{0:T(128)} %param.16) | copy-start | bytes 1252
  0.0 0.7 %copy-start.8 = (f32[104]{0:T(128)S(1)}, f32[104]{0:T(128)}, u32[]{:S(2)}) copy-start(f32[104]{0:T(128)} %param.17) | copy-start | bytes 1252
  0.7 1.2 %copy-start = (f32[9,16384]{1,0:T(8,128)S(1)}, f32[9,16384]{1,0:T(8,128)}, u32[]{:S(2)}) copy-start(f32[9,16384]{1,0:T(8,128)} %cx_hbm.1) | copy-start | bytes 1769476
  1.9 1.2 %copy-start.1 = (f32[9,16384]{1,0:T(8,128)S(1)}, f32[9,16384]{1,0:T(8,128)}, u32[]{:S(2)}) copy-start(f32[9,16384]{1,0:T(8,128)} %cy_hbm.1) | copy-start | bytes 1769476
  3.1 1.1 %copy-start.2 = (f32[1152,128]{1,0:T(8,128)S(1)}, f32[1152,128]{1,0:T(8,128)}, u32[]{:S(2)}) copy-start(f32[1152,128]{1,0:T(8,128)} %x_hbm.1) | copy-start | bytes 1769476
  4.2 1.1 %copy-start.3 = (f32[1152,128]{1,0:T(8,128)S(1)}, f32[1152,128]{1,0:T(8,128)}, u32[]{:S(2)}) copy-start(f32[1152,128]{1,0:T(8,128)} %r_hbm.1) | copy-start | bytes 1769476
  5.3 1.0 %copy-start.4 = (f32[104,1152]{1,0:T(8,128)S(1)}, f32[104,1152]{1,0:T(8,128)}, u32[]{:S(2)}) copy-start(f32[104,1152]{1,0:T(8,128)} %ns_hbm.1) | copy-start | bytes 1437700
  6.3 0.9 %copy-start.5 = (s32[4,16384]{1,0:T(4,128)S(1)}, s32[4,16384]{1,0:T(4,128)}, u32[]{:S(2)}) copy-start(s32[4,16384]{1,0:T(4,128)} %nb_hbm.1) | copy-start | bytes 786436

commit v3 on v2

--- a/solution.py
+++ b/solution.py
@@ -18,7 +18,7 @@
 OWN = 9
 PAD = 16
 STEPS = 136
-UNROLL = 7
+UNROLL = 127
 PARTS = ((0, 4, 5, (3, 1)), (4, 3, 1, (5, 3)), (7, 3, 3, (5, 1)))
 
 
@@ -135,9 +135,9 @@
 
     def steps(group, carry):
         e0m, e0, e1m, e1, e2m, e2, x1, y1, x2, y2 = carry
-        base = pl.multiple_of(group * 72, 8)
-        courant = pl.multiple_of(group * 64, 8)
-        for j in range(8):
+        base = pl.multiple_of(group * 1224, 8)
+        courant = pl.multiple_of(group * 1088, 8)
+        for j in range(136):
             e0p = recv[pl.ds(base + (PAD + 9 * (j + 1)), 8), :]
             x0 = axa[pl.ds(courant + 8 * (j + 2), 8), :]
             y0 = aya[pl.ds(courant + 8 * (j + 2), 8), :]
@@ -148,7 +148,7 @@
             x2, y2, x1, y1 = x1, y1, x0, y0
         return e0m, e0, e1m, e1, e2m, e2, x1, y1, x2, y2
 
-    lax.fori_loop(0, STEPS // 8, steps, (zero, recv[pl.ds(PAD, 8), :]) + (zero,) * 8)
+    lax.fori_loop(0, STEPS // 136, steps, (zero, recv[pl.ds(PAD, 8), :]) + (zero,) * 8)
     groups = DEVICES // 8
     e = [recv[pl.ds(PAD + 8 + 72 * g, 8, stride=OWN), :] for g in range(groups)]
     row = lax.broadcasted_iota(jnp.int32, (8, WIDTH), 0)
@@ -170,12 +170,12 @@
 
 
 def kernel(
-    x_hbm, r_hbm, cx_hbm, cy_hbm, nb_hbm, ns_hbm, owner_hbm, point_hbm, weight_hbm, out, added_hbm, scale_hbm, *scratch
+    x_hbm, r_hbm, cx_hbm, cy_hbm, nb_hbm, ns_hbm, owner_hbm, point_hbm, weight_hbm, out, added, scale, *scratch
 ):
     x, r, cx, cy, nb, ns, owner, point, weight = scratch[:9]
-    tmp, send, recv, back, axa, aya, axb, ayb, added, scale = scratch[9:19]
-    sums, pair, chip, first_in, second_out, second_in = (scratch[19 + 3 * i : 22 + 3 * i] for i in range(6))
-    in_sem, own_sem, send_sem, recv_sem, result_sem, part_send, part_recv = scratch[37:]
+    tmp, send, recv, back, axa, aya, axb, ayb = scratch[9:17]
+    sums, pair, chip, first_in, second_out, second_in = (scratch[17 + 3 * i : 20 + 3 * i] for i in range(6))
+    in_sem, own_sem, send_sem, recv_sem, part_send, part_recv = scratch[35:]
     me = lax.axis_index("pts") * 8 + lax.axis_index("comp")
     loads = [
         pltpu.make_async_copy(a, b, in_sem.at[i])
@@ -302,15 +302,7 @@
                 one = lax.broadcasted_iota(jnp.int32, (8, WIDTH), 1)
                 total = jnp.where(one == 0, v[t : t + 1], jnp.where(one == WIDTH - 1, v[4 + t : 5 + t], 0.0))
                 scale[...] = 1.0 / (1.0 + total)
-    results = [
-        pltpu.make_async_copy(added, added_hbm, result_sem.at[0]),
-        pltpu.make_async_copy(scale, scale_hbm, result_sem.at[1]),
-    ]
-    for c in results:
-        c.start()
     moved.wait_send()
-    for c in results:
-        c.wait()
     own2.wait()
     moved2.wait_send()
     moved2.wait_recv()
@@ -328,13 +320,9 @@
 
     return pl.pallas_call(
         kernel,
-        out_shape=(
-            jax.ShapeDtypeStruct((COMPS, WIDTH), F32),
-            jax.ShapeDtypeStruct((COMPS, WIDTH), F32),
-            jax.ShapeDtypeStruct((8, WIDTH), F32),
-        ),
+        out_shape=(rows(COMPS), rows(COMPS), rows(8)),
         in_specs=[anywhere] * 9,
-        out_specs=(anywhere,) * 3,
+        out_specs=(pl.BlockSpec(memory_space=pltpu.VMEM),) * 3,
         scratch_shapes=[
             *whole,
             rows(8 * NTH),
@@ -345,8 +333,6 @@
             rows(8 * (STEPS + 2)),
             rows(DEVICES),
             rows(DEVICES),
-            rows(COMPS),
-            rows(8),
             *parts(256),
             *parts(128),
             *parts(128),
@@ -357,13 +343,12 @@
             DMA((2,)),
             DMA((2,)),
             DMA((2,)),
-            DMA((2,)),
             DMA((3, 3)),
             DMA((3, 3)),
         ],
         name="timestep",
         compiler_params=pltpu.CompilerParams(
-            collective_id=1, has_side_effects=True, vmem_limit_bytes=48 * 1024 * 1024
+            collective_id=1, has_side_effects=True, vmem_limit_bytes=60 * 1024 * 1024
         ),
     )(*arrays)
 

time: 47.6 us -> 34.6 us (0.73)
  local copies, waits for them, and re-layouts: 7.23 us -> 0.01 us
  Pallas kernels: 39.1 us -> 33.4 us
    unnamed x18 -> x0, local copies, waits for them, and re-layouts: 7.23 us -> none
    pallas_call x1, Pallas kernels: 39.1 us -> 33.4 us  [timestep(): pl.pallas_call(kernel, out_shape=(rows(COMPS), rows(COMPS), rows(8)), in_...]
where the time goes in v3:
time: 34.6 us; the launch traced here: 34.3 us
  Pallas kernels  33.4 us (97%)
  other arithmetic  0.88 us (3%)
    pallas_call x1, Pallas kernels, timestep(): pl.pallas_call(kernel, out_shape=(rows(COMPS), rows(COMPS), rows(8)), in_...  33.4 us
    mul x1, other arithmetic, body(): return (energy + added) * scale[0:1, :]  0.88 us

profile of v3, /device:TPU:1, one launch (start us, length us, event | category | flops | bytes accessed | tf_op | source)
XLA Modules:
  0.0 34.3 jit_solution(4801419881280588624)
XLA Ops:
  0.0 33.4 %timestep.1 = (f32[1152,128]{1,0:T(8,128)S(1)}, f32[1152,128]{1,0:T(8,128)S(1)}, f32[8,128]{1,0:T(8,128)S(1)}) custom-call(f32[1152,128]{1,0:T(8,128)} %x_hbm.1, f32[1152,128]{1,0:T(8,128)} %r_hbm.1, f32[9,16384]{1,0:T(8,128)} %cx_hbm.1, f32[9,16384]{1,0:T(8,128)} %cy_hbm.1, s32[4,16384]{1,0:T(4,128)} %nb_hbm.1, f32[104,1152]{1,0:T(8,128)} %ns_hbm.1, ...), custom_call_target="tpu_custom_call" | custom-call | tf_op jit(solution)/shard_map/timestep/pallas_call | solution.py:321
  33.4 0.9 %add_multiply_fusion = f32[1152,128]{1,0:T(8,128)} fusion(f32[1152,128]{1,0:T(8,128)S(1)} %get-tuple-element.8, f32[1152,128]{1,0:T(8,128)S(1)} %get-tuple-element.9, f32[128]{0:T(128)S(1)} %slice_bitcast_fusion), kind=kLoop, calls=%fused_computation | loop fusion | flops 294912 | bytes 1769984 | tf_op jit(solution)/shard_map/mul | solution.py:369
  (1 shorter events, 0.0 us)

commit v4 on v3

--- a/solution.py
+++ b/solution.py
@@ -16,9 +16,8 @@
 WIDTH = 128
 COMPS = 1152
 OWN = 9
-PAD = 16
-STEPS = 136
-UNROLL = 127
+PAD = 80
+BLOCK = 32
 PARTS = ((0, 4, 5, (3, 1)), (4, 3, 1, (5, 3)), (7, 3, 3, (5, 1)))
 
 
@@ -28,23 +27,6 @@
 
 def digit(index, bit):
     return (index >> bit) & 3
-
-
-def each_peer(body):
-    def some(j, carry):
-        for q in range(UNROLL):
-            body(DEVICES - 1 - (j * UNROLL + q))
-        return carry
-
-    whole = (DEVICES - 1) // UNROLL
-    lax.fori_loop(0, whole, some, 0)
-    for i in range(DEVICES - 1 - whole * UNROLL, 0, -1):
-        body(i)
-
-
-def far_first(i):
-    high, low = i & 0b1010100, i & 0b0101010
-    return (low << 1) | ((high >> 1) ^ low) | (i & 1)
 
 
 def refract(x, r, tmp, send):
@@ -106,9 +88,9 @@
     lane = lax.broadcasted_iota(jnp.int32, (4, WIDTH), 1)
     side = lax.broadcasted_iota(jnp.int32, (4, WIDTH), 0)
     shift = lane + jnp.where(side == 0, -1, jnp.where(side == 1, 1, jnp.where(side == 2, -WIDTH, WIDTH)))
-    for a in (axa, aya):
-        a[pl.ds(0, 16), :] = jnp.zeros((16, WIDTH), F32)
-        a[pl.ds(16 + 8 * DEVICES, 8 * (STEPS - DEVICES)), :] = jnp.zeros((8 * (STEPS - DEVICES), WIDTH), F32)
+    for a, edge in ((axa, 16), (aya, 16), (axb, 8), (ayb, 8)):
+        a[pl.ds(0, edge), :] = jnp.zeros((edge, WIDTH), F32)
+        a[pl.ds(a.shape[0] - edge, edge), :] = jnp.zeros((edge, WIDTH), F32)
 
     @pl.loop(0, DEVICES // 8)
     def _(group):
@@ -121,7 +103,7 @@
                 v = c[pl.ds(0, 8), columns]
                 a[pl.ds(pl.multiple_of((s + 2) * 8, 8), 8), :] = v * jnp.where(v > 0, up, down)
                 v = c[pl.ds(8, 1), columns]
-                b[pl.ds(pl.multiple_of(group * 8, 8) + j, 1), :] = v * jnp.where(v > 0, up, down)
+                b[pl.ds(pl.multiple_of(group * 8, 8) + (8 + j), 1), :] = v * jnp.where(v > 0, up, down)
 
 
 def upwind(e, south, north, vx, vy):
@@ -130,27 +112,29 @@
     return out - jnp.abs(vy) * (e - jnp.where(vy > 0, south, north))
 
 
-def advect(recv, back, axa, aya, axb, ayb):
-    zero = jnp.zeros((8, WIDTH), F32)
-
-    def steps(group, carry):
-        e0m, e0, e1m, e1, e2m, e2, x1, y1, x2, y2 = carry
-        base = pl.multiple_of(group * 1224, 8)
-        courant = pl.multiple_of(group * 1088, 8)
-        for j in range(136):
-            e0p = recv[pl.ds(base + (PAD + 9 * (j + 1)), 8), :]
-            x0 = axa[pl.ds(courant + 8 * (j + 2), 8), :]
-            y0 = aya[pl.ds(courant + 8 * (j + 2), 8), :]
-            e1p = upwind(e0, e0m, e0p, x0, y0)
-            e2p = upwind(e1, e1m, e1p, x1, y1)
-            back[pl.ds(base + (24 + 9 * (j - 2)), 8), :] = upwind(e2, e2m, e2p, x2, y2)
-            e0m, e0, e1m, e1, e2m, e2 = e0, e0p, e1, e1p, e2, e2p
-            x2, y2, x1, y1 = x1, y1, x0, y0
-        return e0m, e0, e1m, e1, e2m, e2, x1, y1, x2, y2
-
-    lax.fori_loop(0, STEPS // 136, steps, (zero, recv[pl.ds(PAD, 8), :]) + (zero,) * 8)
-    groups = DEVICES // 8
-    e = [recv[pl.ds(PAD + 8 + 72 * g, 8, stride=OWN), :] for g in range(groups)]
+def advect(block, recv, back, axa, aya, axb, ayb):
+    base = pl.multiple_of(block * (BLOCK * OWN), 8)
+    low = pl.multiple_of(block * (BLOCK * 8), 8)
+
+    def courants(s):
+        rows = pl.ds(low + 8 * (s + 2), 8)
+        return axa[rows, :], aya[rows, :]
+
+    def first(s):
+        return recv[pl.ds(base + (PAD + OWN * s), 8), :]
+
+    e0, e1, e2, c = {-3: first(-3), -2: first(-2)}, {}, {}, {}
+    for s in range(-2, BLOCK + 2):
+        e0[s + 1], c[s] = first(s + 1), courants(s)
+        e1[s] = upwind(e0[s], e0[s - 1], e0[s + 1], *c[s])
+        if s >= 0:
+            e2[s - 1] = upwind(e1[s - 1], e1[s - 2], e1[s], *c[s - 1])
+        if s >= 2:
+            back[pl.ds(base + OWN * (s - 2), 8), :] = upwind(e2[s - 2], e2[s - 3], e2[s - 1], *c[s - 2])
+    groups = BLOCK // 8 + 2
+    last = groups - 1
+    e = [recv[pl.ds(base + (PAD + 8 + 72 * (g - 1)), 8, stride=OWN), :] for g in range(groups)]
+    courant = pl.multiple_of(block * BLOCK, 8)
     row = lax.broadcasted_iota(jnp.int32, (8, WIDTH), 0)
     for _ in range(3):
         up = [pltpu.roll(v, 1, 0) for v in e]
@@ -158,21 +142,21 @@
         e = [
             upwind(
                 e[g],
-                jnp.where(row == 0, up[g - 1], up[g]),
-                jnp.where(row == 7, down[(g + 1) % groups], down[g]),
-                axb[pl.ds(8 * g, 8), :],
-                ayb[pl.ds(8 * g, 8), :],
+                jnp.where(row == 0, up[max(g - 1, 0)], up[g]),
+                jnp.where(row == 7, down[min(g + 1, last)], down[g]),
+                axb[pl.ds(courant + 8 * g, 8), :],
+                ayb[pl.ds(courant + 8 * g, 8), :],
             )
             for g in range(groups)
         ]
-    for g in range(groups):
-        back[pl.ds(24 + 8 + 72 * g, 8, stride=OWN), :] = e[g]
+    for g in range(1, last):
+        back[pl.ds(base + (8 + 72 * (g - 1)), 8, stride=OWN), :] = e[g]
 
 
 def kernel(
     x_hbm, r_hbm, cx_hbm, cy_hbm, nb_hbm, ns_hbm, owner_hbm, point_hbm, weight_hbm, out, added, scale, *scratch
 ):
-    x, r, cx, cy, nb, ns, owner, point, weight = scratch[:9]
+    spec, r, cx, cy, nb, ns, owner, point, weight = scratch[:9]
     tmp, send, recv, back, axa, aya, axb, ayb = scratch[9:17]
     sums, pair, chip, first_in, second_out, second_in = (scratch[17 + 3 * i : 20 + 3 * i] for i in range(6))
     in_sem, own_sem, send_sem, recv_sem, part_send, part_recv = scratch[35:]
@@ -181,7 +165,7 @@
         pltpu.make_async_copy(a, b, in_sem.at[i])
         for i, (a, b) in enumerate(
             (
-                (x_hbm, x),
+                (x_hbm, spec),
                 (r_hbm, r),
                 (ns_hbm, ns),
                 (owner_hbm, owner),
@@ -196,51 +180,48 @@
     for c in loads:
         c.start()
     barrier = pltpu.get_barrier_semaphore()
-    each_peer(lambda i: pl.semaphore_signal(barrier, inc=1, **at(me ^ i)))
+    for i in range(DEVICES - 1, 0, -1):
+        pl.semaphore_signal(barrier, inc=1, **at(me ^ i))
 
     recv[pl.ds(0, PAD), :] = jnp.zeros((PAD, WIDTH), F32)
-    tail = recv.shape[0] - PAD - COMPS
-    recv[pl.ds(PAD + COMPS, tail), :] = jnp.zeros((tail, WIDTH), F32)
+    recv[pl.ds(PAD + COMPS, PAD), :] = jnp.zeros((PAD, WIDTH), F32)
     loads[0].wait()
     loads[1].wait()
-    refract(x, r, tmp, send)
+    refract(spec, r, tmp, send)
     for c in loads[2:6]:
         c.wait()
     local_sums(ns, owner, point, weight, sums)
     pl.semaphore_wait(barrier, DEVICES - 1)
 
-    def over(stage, p, ref, source, target, device):
+    def over(stage, p, source, target, device):
         return pltpu.make_async_remote_copy(source, target, part_send.at[stage, p], part_recv.at[stage, p], **at(device))
 
     def wait_part(stage, p, ref):
-        w = over(stage, p, ref, ref, ref, me)
+        w = over(stage, p, ref, ref, me)
         w.wait_recv()
         w.wait_send()
 
     for p in range(3):
         other = pl.ds(pl.multiple_of((1 - me % 2) * 128, 128), 128)
-        over(0, p, None, sums[p].at[other], pair[p], me ^ 1).start()
-
-    def transpose(stage, source, target, source_at, target_at):
-        def start(i):
-            to = me ^ far_first(i)
-            pltpu.make_async_remote_copy(
-                source.at[pl.ds(source_at + to * OWN, OWN)],
-                target.at[pl.ds(target_at + me * OWN, OWN)],
-                send_sem.at[stage],
-                recv_sem.at[stage],
-                **at(to),
-            ).start()
-
-        each_peer(start)
-        own = pltpu.make_async_copy(
-            source.at[pl.ds(source_at + me * OWN, OWN)], target.at[pl.ds(target_at + me * OWN, OWN)], own_sem.at[stage]
-        )
-        own.start()
-        rest = recv.at[pl.ds(0, (DEVICES - 1) * OWN)]
-        return own, pltpu.make_async_remote_copy(rest, rest, send_sem.at[stage], recv_sem.at[stage], **at(me))
-
-    own, moved = transpose(0, send, recv, 0, PAD)
+        over(0, p, sums[p].at[other], pair[p], me ^ 1).start()
+
+    x = me // BLOCK
+
+    def send_block(source, target, send_at, recv_at, shift, to):
+        pltpu.make_async_remote_copy(
+            source.at[pl.ds(to * OWN, OWN)], target.at[pl.ds(shift + me * OWN, OWN)], send_at, recv_at, **at(to)
+        ).start()
+
+    def wait_blocks(n, semaphore):
+        some = recv.at[pl.ds(0, n * OWN)]
+        return pltpu.make_async_remote_copy(some, some, semaphore, semaphore, **at(me))
+
+    for i in range(DEVICES - 1, 0, -1):
+        send_block(send, recv, send_sem.at[0], recv_sem.at[i // BLOCK], PAD, me ^ i)
+    own = pltpu.make_async_copy(
+        send.at[pl.ds(me * OWN, OWN)], recv.at[pl.ds(PAD + me * OWN, OWN)], own_sem.at[0]
+    )
+    own.start()
 
     for p, (first, tiles, bit, _) in enumerate(PARTS):
         wait_part(0, p, pair[p])
@@ -249,16 +230,34 @@
         for d in range(1, 4):
             to = me ^ (d << bit)
             block = pl.ds(pl.multiple_of(digit(to, bit) * 32, 32), 32)
-            over(1, p, None, chip[p].at[block], first_in[p].at[pl.ds((d - 1) * 32, 32)], to).start()
+            over(1, p, chip[p].at[block], first_in[p].at[pl.ds((d - 1) * 32, 32)], to).start()
 
     for c in loads[6:]:
         c.wait()
     prepare(cx, cy, nb, axa, aya, axb, ayb)
+
+    def propagate(block):
+        advect(block, recv, back, axa, aya, axb, ayb)
+        for i in range(BLOCK - 1, 0, -1):
+            send_block(back, out, send_sem.at[1], recv_sem.at[4], 0, block * BLOCK + (me % BLOCK) ^ i)
+
+    half = x // 2
+    wait_blocks(BLOCK, recv_sem.at[3]).wait_recv()
+    wait_blocks(BLOCK, recv_sem.at[2]).wait_recv()
+    propagate(3 * (1 - half))
+    send_block(back, out, send_sem.at[1], recv_sem.at[4], 0, 3 * (1 - half) * BLOCK + me % BLOCK)
+    wait_blocks(BLOCK, recv_sem.at[1]).wait_recv()
     own.wait()
-    moved.wait_recv()
-    advect(recv, back, axa, aya, axb, ayb)
-    own2, moved2 = transpose(1, back, out, 24, 0)
-
+    wait_blocks(BLOCK - 1, recv_sem.at[0]).wait_recv()
+    own2 = pltpu.make_async_copy(back.at[pl.ds(me * OWN, OWN)], out.at[pl.ds(me * OWN, OWN)], own_sem.at[1])
+
+    def two(b, carry):
+        block = (1 - b) * (2 - half) + b * (x + 1 - 2 * (x % 2))
+        propagate(block)
+        send_block(back, out, send_sem.at[1], recv_sem.at[4], 0, block * BLOCK + me % BLOCK)
+        return carry
+
+    lax.fori_loop(0, 2, two, 0)
     for p, (first, tiles, bit, (b1, b2)) in enumerate(PARTS):
         wait_part(1, p, first_in[p])
         block = pl.ds(pl.multiple_of(digit(me, bit) * 32, 32), 32)
@@ -272,19 +271,17 @@
                 v = jnp.zeros((32, WIDTH), F32)
             second_out[p][pl.ds(t, 32, stride=4), :] = v
 
-        @pl.loop(1, 16)
-        def _(q):
-            to = me ^ (((q >> 2) << b1) | ((q & 3) << b2))
-            block = digit(to, b1) * 4 + digit(to, b2)
+        mine = digit(me, b1) * 4 + digit(me, b2)
+        for q in range(15, 0, -1):
             over(
                 2,
                 p,
-                None,
-                second_out[p].at[pl.ds(pl.multiple_of(block * 8, 8), 8)],
-                second_in[p].at[pl.ds(pl.multiple_of(q * 8, 8), 8)],
-                to,
+                second_out[p].at[pl.ds(pl.multiple_of((mine ^ q) * 8, 8), 8)],
+                second_in[p].at[pl.ds(q * 8, 8)],
+                me ^ (((q >> 2) << b1) | ((q & 3) << b2)),
             ).start()
-
+    propagate(x)
+    own2.start()
     lane = lax.broadcasted_iota(jnp.int32, (WIDTH, WIDTH), 1)
     for p, (first, tiles, bit, (b1, b2)) in enumerate(PARTS):
         wait_part(2, p, second_in[p].at[pl.ds(8, 120)])
@@ -302,10 +299,10 @@
                 one = lax.broadcasted_iota(jnp.int32, (8, WIDTH), 1)
                 total = jnp.where(one == 0, v[t : t + 1], jnp.where(one == WIDTH - 1, v[4 + t : 5 + t], 0.0))
                 scale[...] = 1.0 / (1.0 + total)
-    moved.wait_send()
+    wait_blocks(DEVICES - 1, send_sem.at[0]).wait_send()
     own2.wait()
-    moved2.wait_send()
-    moved2.wait_recv()
+    wait_blocks(DEVICES - 1, send_sem.at[1]).wait_send()
+    wait_blocks(DEVICES - 1, recv_sem.at[4]).wait_recv()
 
 
 def timestep(*arrays):
@@ -327,12 +324,12 @@
             *whole,
             rows(8 * NTH),
             rows(COMPS),
-            rows(PAD + OWN * (STEPS + 2)),
-            rows(24 + OWN * STEPS),
-            rows(8 * (STEPS + 2)),
-            rows(8 * (STEPS + 2)),
-            rows(DEVICES),
-            rows(DEVICES),
+            rows(PAD + COMPS + PAD),
+            rows(COMPS),
+            rows(8 * (DEVICES + 4)),
+            rows(8 * (DEVICES + 4)),
+            rows(DEVICES + 16),
+            rows(DEVICES + 16),
             *parts(256),
             *parts(128),
             *parts(128),
@@ -342,7 +339,7 @@
             DMA((9,)),
             DMA((2,)),
             DMA((2,)),
-            DMA((2,)),
+            DMA((5,)),
             DMA((3, 3)),
             DMA((3, 3)),
         ],

time: 34.6 us -> 33.7 us (0.974)
  Pallas kernels: 33.4 us -> 32.7 us
    pallas_call x1, Pallas kernels: 33.4 us -> 32.7 us  [timestep(): pl.pallas_call(kernel, out_shape=(rows(COMPS), rows(COMPS), rows(8)), in_...]
where the time goes in v4:
time: 33.7 us; the launch traced here: 33.6 us
  Pallas kernels  32.7 us (97%)
  other arithmetic  0.88 us (3%)
    pallas_call x1, Pallas kernels, timestep(): pl.pallas_call(kernel, out_shape=(rows(COMPS), rows(COMPS), rows(8)), in_...  32.7 us
    mul x1, other arithmetic, body(): return (energy + added) * scale[0:1, :]  0.88 us

profile of v4, /device:TPU:1, one launch (start us, length us, event | category | flops | bytes accessed | tf_op | source)
XLA Modules:
  0.0 33.6 jit_solution(2090441650149932493)
XLA Ops:
  0.0 32.7 %timestep.1 = (f32[1152,128]{1,0:T(8,128)S(1)}, f32[1152,128]{1,0:T(8,128)S(1)}, f32[8,128]{1,0:T(8,128)S(1)}) custom-call(f32[1152,128]{1,0:T(8,128)} %x_hbm.1, f32[1152,128]{1,0:T(8,128)} %r_hbm.1, f32[9,16384]{1,0:T(8,128)} %cx_hbm.1, f32[9,16384]{1,0:T(8,128)} %cy_hbm.1, s32[4,16384]{1,0:T(4,128)} %nb_hbm.1, f32[104,1152]{1,0:T(8,128)} %ns_hbm.1, ...), custom_call_target="tpu_custom_call" | custom-call | tf_op jit(solution)/shard_map/timestep/pallas_call | solution.py:318
  32.7 0.9 %add_multiply_fusion = f32[1152,128]{1,0:T(8,128)} fusion(f32[1152,128]{1,0:T(8,128)S(1)} %get-tuple-element.8, f32[1152,128]{1,0:T(8,128)S(1)} %get-tuple-element.9, f32[128]{0:T(128)S(1)} %slice_bitcast_fusion), kind=kLoop, calls=%fused_computation | loop fusion | flops 294912 | bytes 1769984 | tf_op jit(solution)/shard_map/mul | solution.py:366
  (1 shorter events, 0.0 us)

commit v5 on v4

--- a/solution.py
+++ b/solution.py
@@ -177,20 +177,19 @@
             )
         )
     ]
-    for c in loads:
+    for c in loads[:2]:
         c.start()
     barrier = pltpu.get_barrier_semaphore()
     for i in range(DEVICES - 1, 0, -1):
         pl.semaphore_signal(barrier, inc=1, **at(me ^ i))
 
+    for c in loads[2:]:
+        c.start()
     recv[pl.ds(0, PAD), :] = jnp.zeros((PAD, WIDTH), F32)
     recv[pl.ds(PAD + COMPS, PAD), :] = jnp.zeros((PAD, WIDTH), F32)
     loads[0].wait()
     loads[1].wait()
     refract(spec, r, tmp, send)
-    for c in loads[2:6]:
-        c.wait()
-    local_sums(ns, owner, point, weight, sums)
     pl.semaphore_wait(barrier, DEVICES - 1)
 
     def over(stage, p, source, target, device):
@@ -200,10 +199,6 @@
         w = over(stage, p, ref, ref, me)
         w.wait_recv()
         w.wait_send()
-
-    for p in range(3):
-        other = pl.ds(pl.multiple_of((1 - me % 2) * 128, 128), 128)
-        over(0, p, sums[p].at[other], pair[p], me ^ 1).start()
 
     x = me // BLOCK
 
@@ -222,6 +217,13 @@
         send.at[pl.ds(me * OWN, OWN)], recv.at[pl.ds(PAD + me * OWN, OWN)], own_sem.at[0]
     )
     own.start()
+
+    for c in loads[2:6]:
+        c.wait()
+    local_sums(ns, owner, point, weight, sums)
+    for p in range(3):
+        other = pl.ds(pl.multiple_of((1 - me % 2) * 128, 128), 128)
+        over(0, p, sums[p].at[other], pair[p], me ^ 1).start()
 
     for p, (first, tiles, bit, _) in enumerate(PARTS):
         wait_part(0, p, pair[p])

time: 33.7 us -> 33.6 us (level)
  no operation moved by 1% of the time
where the time goes in v5:
time: 33.6 us; the launch traced here: 33.5 us
  Pallas kernels  32.6 us (97%)
  other arithmetic  0.88 us (3%)
    pallas_call x1, Pallas kernels, timestep(): pl.pallas_call(kernel, out_shape=(rows(COMPS), rows(COMPS), rows(8)), in_...  32.6 us
    mul x1, other arithmetic, body(): return (energy + added) * scale[0:1, :]  0.88 us

profile of v5, /device:TPU:1, one launch (start us, length us, event | category | flops | bytes accessed | tf_op | source)
XLA Modules:
  0.0 33.5 jit_solution(3291232918749669802)
XLA Ops:
  0.0 32.6 %timestep.1 = (f32[1152,128]{1,0:T(8,128)S(1)}, f32[1152,128]{1,0:T(8,128)S(1)}, f32[8,128]{1,0:T(8,128)S(1)}) custom-call(f32[1152,128]{1,0:T(8,128)} %x_hbm.1, f32[1152,128]{1,0:T(8,128)} %r_hbm.1, f32[9,16384]{1,0:T(8,128)} %cx_hbm.1, f32[9,16384]{1,0:T(8,128)} %cy_hbm.1, s32[4,16384]{1,0:T(4,128)} %nb_hbm.1, f32[104,1152]{1,0:T(8,128)} %ns_hbm.1, ...), custom_call_target="tpu_custom_call" | custom-call | tf_op jit(solution)/shard_map/timestep/pallas_call | solution.py:320
  32.6 0.9 %add_multiply_fusion = f32[1152,128]{1,0:T(8,128)} fusion(f32[1152,128]{1,0:T(8,128)S(1)} %get-tuple-element.8, f32[1152,128]{1,0:T(8,128)S(1)} %get-tuple-element.9, f32[128]{0:T(128)S(1)} %slice_bitcast_fusion), kind=kLoop, calls=%fused_computation | loop fusion | flops 294912 | bytes 1769984 | tf_op jit(solution)/shard_map/mul | solution.py:368
  (1 shorter events, 0.0 us)

commit v6 on v4

--- a/solution.py
+++ b/solution.py
@@ -27,6 +27,10 @@
 
 def digit(index, bit):
     return (index >> bit) & 3
+
+
+def hops(i):
+    return sum(min(digit(i, bit), 4 - digit(i, bit)) for bit in (1, 3, 5))
 
 
 def refract(x, r, tmp, send):
@@ -216,7 +220,7 @@
         some = recv.at[pl.ds(0, n * OWN)]
         return pltpu.make_async_remote_copy(some, some, semaphore, semaphore, **at(me))
 
-    for i in range(DEVICES - 1, 0, -1):
+    for i in sorted(range(1, DEVICES), key=lambda i: (-(i // BLOCK), -hops(i), -i)):
         send_block(send, recv, send_sem.at[0], recv_sem.at[i // BLOCK], PAD, me ^ i)
     own = pltpu.make_async_copy(
         send.at[pl.ds(me * OWN, OWN)], recv.at[pl.ds(PAD + me * OWN, OWN)], own_sem.at[0]

time: 33.7 us -> 33.5 us (level)
  no operation moved by 1% of the time
where the time goes in v6:
time: 33.5 us; the launch traced here: 33.4 us
  Pallas kernels  32.5 us (97%)
  other arithmetic  0.88 us (3%)
    pallas_call x1, Pallas kernels, timestep(): pl.pallas_call(kernel, out_shape=(rows(COMPS), rows(COMPS), rows(8)), in_...  32.5 us
    mul x1, other arithmetic, body(): return (energy + added) * scale[0:1, :]  0.88 us

profile of v6, /device:TPU:1, one launch (start us, length us, event | category | flops | bytes accessed | tf_op | source)
XLA Modules:
  0.0 33.4 jit_solution(83433015319817191)
XLA Ops:
  0.0 32.5 %timestep.1 = (f32[1152,128]{1,0:T(8,128)S(1)}, f32[1152,128]{1,0:T(8,128)S(1)}, f32[8,128]{1,0:T(8,128)S(1)}) custom-call(f32[1152,128]{1,0:T(8,128)} %x_hbm.1, f32[1152,128]{1,0:T(8,128)} %r_hbm.1, f32[9,16384]{1,0:T(8,128)} %cx_hbm.1, f32[9,16384]{1,0:T(8,128)} %cy_hbm.1, s32[4,16384]{1,0:T(4,128)} %nb_hbm.1, f32[104,1152]{1,0:T(8,128)} %ns_hbm.1, ...), custom_call_target="tpu_custom_call" | custom-call | tf_op jit(solution)/shard_map/timestep/pallas_call | solution.py:322
  32.5 0.9 %add_multiply_fusion = f32[1152,128]{1,0:T(8,128)} fusion(f32[1152,128]{1,0:T(8,128)S(1)} %get-tuple-element.8, f32[1152,128]{1,0:T(8,128)S(1)} %get-tuple-element.9, f32[128]{0:T(128)S(1)} %slice_bitcast_fusion), kind=kLoop, calls=%fused_computation | loop fusion | flops 294912 | bytes 1769984 | tf_op jit(solution)/shard_map/mul | solution.py:370
  (1 shorter events, 0.0 us)
